TPU v7x, 32 devices: a whole 2x2x4 slice. The times are simulated.
32 devices in a mesh: sec: 2 (over core), dom: 16 (over z, y, x).
Axes of the slice: x: 2, y: 2, z: 4, core: 2. Of those that a mesh axis runs over, the one named last changes fastest.
Arguments:
- state: float32 [3, 8, 262144], P(None, None, ('sec', 'dom')), may hold values from -6 to 6
- send_rows: int32 [524288], P(('sec', 'dom')), may hold values from 0 to 8191, as said below
- intersection_source: int32 [524288], P(('sec', 'dom')), may hold values from 0 to 16383, as said below
- intersection_weight: float32 [524288], P(('sec', 'dom')), may hold values from 0.1 to 1
- couple_rate: float32 [2, 3], P('sec'), may hold values from 0.2 to 0.8
- atm_metric: float32 [2, 131072], P(None, 'dom'), may hold values from 0.5 to 2
- wave_speed: float32 [8], replicated, may hold values from 0.5 to 2
- ocean_adjacent: int32 [6, 131072], P(None, 'dom'), may hold values from 0 to 9215, as said below
- ocean_edges: int32 [2, 8192], P(None, 'dom'), may hold values from 0 to 8191, as said below
- ocean_kappa: float32 [131072], P('dom'), may hold values from 0.02 to 0.15
Outputs:
- new_state: float32 [3, 8, 262144], P(None, None, ('sec', 'dom'))
Inputs may be any that keep to these rules, and one draw needn't show every extreme that they name: `send_rows`: the ocean's band runs across the atmosphere's, so every block intersects every block of the other section. Within a block, cut the rows into 16 strips of 512 rows by position across the band; the 1024 slots for peer p hold the rows of strips p, p + 1, ... (modulo 16), 2 strips in all, in an order drawn from the seed; so every row fills exactly 2 slots. `intersection_source`: in each block a permutation of all 16384 received slots; the entries 2 * r .. 2 * r + 1 belong to row r. `ocean_adjacent`: each cell's neighbours on a hexagonal grid in its block's own row order; values from 8192 on name rim slots (first the cells of the previous block's last column, then those of the next block's first column, by position across the band); a cell at the band's edge names itself for a missing neighbour. `ocean_edges`: ordered by position across the band.
All inputs are finite; a program needn't handle non-finite values.
Results may differ from a plain program's by a relative error of at most 0.0001.
Values sent between devices are 32-bit elements; how exact they have to be, the bound alone decides.
A program may use at most 128 MiB of HBM per device.

v0:
```python
import jax
import jax.numpy as jnp
import numpy as np
from jax import lax
from jax.sharding import PartitionSpec as P

INTERSECTIONS = 2


TIME_STEP = 0.05


def extended_2(shard, sides, width):
    for axis, dim in sides:
        size, length = (lax.axis_size(axis), shard.shape[dim])
        up = [(i, (i + 1) % size) for i in range(size)]
        down = [(j, i) for i, j in up]
        last = lax.slice_in_dim(shard, length - width, length, axis=dim)
        leading = lax.slice_in_dim(shard, 0, width, axis=dim)
        before = lax.ppermute(last, axis, up)
        after = lax.ppermute(leading, axis, down)
        shard = jnp.concatenate([before, shard, after], axis=dim)
    return shard


def gll_derivative():
    nodes = np.array([-1.0, -1.0 / np.sqrt(5.0), 1.0 / np.sqrt(5.0), 1.0])
    barycentric = np.array(
        [
            1.0 / np.prod([nodes[first] - nodes[second] for second in range(4) if second != first])
            for first in range(4)
        ]
    )
    matrix = np.zeros((4, 4))
    for first in range(4):
        for second in range(4):
            if first != second:
                matrix[first, second] = (
                    barycentric[second] / barycentric[first] / (nodes[first] - nodes[second])
                )
        matrix[first, first] = -np.sum(matrix[first])
    return jnp.asarray(matrix, jnp.float32)


def along_first(field, derivative):
    depth, across, along = field.shape
    grouped = field.reshape(depth, across // 4, 4, along)
    return jnp.einsum(
        "ij,lejy->leiy", derivative, grouped, precision=lax.Precision.HIGHEST
    ).reshape(field.shape)


def along_second(field, derivative):
    depth, across, along = field.shape
    grouped = field.reshape(depth, across, along // 4, 4)
    return jnp.einsum(
        "ij,lxej->lxei", derivative, grouped, precision=lax.Precision.HIGHEST
    ).reshape(field.shape)


def dycore(fields, metric_x, metric_y, speeds):
    derivative = gll_derivative()
    eastward, northward, geopotential = (fields[0], fields[1], fields[2])
    slope_x = metric_x * along_first(geopotential, derivative)
    slope_y = metric_y * along_second(geopotential, derivative)
    spread = metric_x * along_first(eastward, derivative) + metric_y * along_second(
        northward, derivative
    )
    return jnp.stack(
        [
            eastward - TIME_STEP * slope_x,
            northward - TIME_STEP * slope_y,
            geopotential - TIME_STEP * speeds[:, None, None] * spread,
        ]
    )


def average_first(fields, before, after):
    phase = (jnp.arange(fields.shape[2]) % 4)[:, None]
    return jnp.where(
        phase == 3, (fields + after) * 0.5, jnp.where(phase == 0, (fields + before) * 0.5, fields)
    )


def average_second(fields):
    along = fields.shape[3]
    position = jnp.arange(along)
    phase = position % 4
    after = jnp.roll(fields, -1, axis=3)
    before = jnp.roll(fields, 1, axis=3)
    joined_after = (phase == 3) & (position < along - 1)
    joined_before = (phase == 0) & (position > 0)
    return jnp.where(
        joined_after,
        (fields + after) * 0.5,
        jnp.where(joined_before, (fields + before) * 0.5, fields),
    )


def body(
    state,
    send_rows,
    intersection_source,
    intersection_weight,
    couple_rate,
    atm_metric,
    wave_speed,
    ocean_adjacent,
    ocean_edges,
    ocean_kappa,
):
    levels = state.shape[1]
    y_points = ocean_edges.shape[1]
    x_points = state.shape[2] // y_points
    section = lax.axis_index("sec")
    atmosphere = section == 0
    surface = state[:, levels - 1]
    outgoing = surface[:, send_rows]
    slot_count = outgoing.shape[1]
    blank = jnp.zeros_like(outgoing)
    spread_out = jnp.where(
        atmosphere,
        jnp.concatenate([blank, outgoing], axis=1),
        jnp.concatenate([outgoing, blank], axis=1),
    )
    arrived = lax.all_to_all(spread_out, ("sec", "dom"), split_axis=1, concat_axis=1, tiled=True)
    incoming = lax.dynamic_slice_in_dim(arrived, (1 - section) * slot_count, slot_count, 1)
    weights = intersection_weight.reshape(-1, INTERSECTIONS)
    values = incoming[:, intersection_source].reshape(3, -1, INTERSECTIONS)
    regrid = jnp.sum(values * weights, axis=-1) / jnp.sum(weights, axis=-1)
    metric = atm_metric.reshape(2, x_points, y_points)

    def advance(current):
        grid = current.reshape(3, levels, x_points, y_points)
        return dycore(grid, metric[0], metric[1], wave_speed).reshape(current.shape)

    def unchanged(current):
        return current

    segmented = lax.cond(atmosphere, advance, unchanged, state)
    positions = jnp.arange(y_points, dtype=jnp.int32)
    left_rows = jnp.where(atmosphere, positions, ocean_edges[0])
    right_rows = jnp.where(atmosphere, (x_points - 1) * y_points + positions, ocean_edges[1])
    border = jnp.stack([segmented[:, :, left_rows], segmented[:, :, right_rows]], axis=2)
    rimmed = extended_2(border, (("dom", 2),), 1)
    western = rimmed[:, :, 0]
    eastern = rimmed[:, :, 3]

    def finish_atmosphere(operands):
        current, west_side, east_side = operands
        grid = current.reshape(3, levels, x_points, y_points)
        padded = jnp.concatenate([west_side[:, :, None], grid, east_side[:, :, None]], axis=2)
        averaged = average_second(average_first(grid, padded[:, :, :-2], padded[:, :, 2:]))
        return averaged.reshape(current.shape)

    def sweep_ocean(operands):
        current, west_side, east_side = operands
        extended = jnp.concatenate([current, west_side, east_side], axis=2)
        summed = jnp.zeros_like(current)
        for neighbor in range(6):
            summed = summed + (extended[:, :, ocean_adjacent[neighbor]] - current)
        return current + ocean_kappa * summed

    updated = lax.cond(atmosphere, finish_atmosphere, sweep_ocean, (segmented, western, eastern))
    rates = couple_rate[0][:, None]
    surface_top = updated[:, levels - 1]
    surface_top = surface_top + rates * (regrid - surface_top)
    return updated.at[:, levels - 1].set(surface_top)


def solution(mesh):
    in_specs = (
        P(None, None, ("sec", "dom")),
        P(("sec", "dom")),
        P(("sec", "dom")),
        P(("sec", "dom")),
        P("sec", None),
        P(None, "dom"),
        P(),
        P(None, "dom"),
        P(None, "dom"),
        P("dom"),
    )
    out_specs = P(None, None, ("sec", "dom"))
    return jax.shard_map(body, mesh=mesh, in_specs=in_specs, out_specs=out_specs, check_vma=False)
```

profile of v0, /device:TPU:1, one launch (start us, length us, event | category | flops | bytes accessed | tf_op | source)
XLA Modules:
  0.0 745.3 jit_solution(7190524143693755592)
XLA Ops:
  0.0 1.1 copy.204
  1.1 0.1 slice.134
  1.2 2.6 copy.190
  3.8 0.9 fusion.26
  4.7 56.6 %gather_fusion.8 = f32[16384,3]{1,0:T(8,128)} fusion(f32[3,8192]{0,1:T(8,128)} %bitcast.117, s32[16384]{0:T(1024)S(1)} %fusion.26), kind=kCustom, calls=%fused_computation.8 | custom fusion | bytes 458752 | tf_op jit(solution)/shard_map/gather | solution.py:118
  61.4 16.0 %pad_select_fusion = f32[3,32768]{0,1:T(8,128)} fusion(f32[3,16384]{0,1:T(8,128)} %bitcast.119, pred[]{:T(512)S(6)} %eq.33), kind=kLoop, calls=%fused_computation.75 | loop fusion | flops 98304 | bytes 589825 | tf_op jit(solution)/shard_map/jit(_where)/select_n | solution.py:121
  77.4 9.9 %copy.184 = f32[3,32,1024]{2,0,1:T(4,128)} copy(f32[3,32,1024]{0,2,1:T(8,128)} %bitcast.109) | data formatting | bytes 786432 | tf_op jit(solution)/shard_map/all_to_all | solution.py:126
  87.3 7.2 all-to-all-start
  94.5 0.0 copy-start.3
  94.5 0.0 copy-start.1
  94.5 0.0 copy-start
  94.5 0.0 copy-start.4
  94.5 10.6 %copy.176 = f32[3,8,8192]{1,0,2:T(4,128)} copy(f32[3,8,8192]{2,1,0:T(8,128)S(1)} %get-tuple-element.175) | data formatting | bytes 1572864 | tf_op jit(solution)/shard_map/cond | solution.py:140
  105.1 7.3 gather_fusion.7
  112.4 0.3 copy.179
  112.6 5.3 collective-permute-start.1
  117.9 7.3 gather_fusion.6
  125.2 0.3 copy.177
  125.5 0.0 collective-permute-start
  125.6 5.5 mul.165
  131.1 3.3 reduce_sum.22
  134.4 0.0 collective-permute-done.1
  134.5 482.7 %conditional.3 = (f32[3,8,8192]{2,1,0:T(8,128)}) conditional(s32[]{:T(128)} %convert_element_type.4, (f32[8192]{0:T(1024)S(1)}, f32[3,8,1,512]{3,1,2,0:T(8,128)S(1)}, f32[3,8,1,512]{3,1,2,0:T(8,128)S(1)}, f32[3,8,8192]{2,1,0:T(8,128)S(1)}, s32[6,8192]{1,0:T(8,128)S(1)}) %tuple.75, (f32[3,8,8192]{2,1,0:T(8,128)S(1)}, f32[3,8,1,512]{3,1,2,0:T(8,128)S(1)}, ...), branch_computations={%region_2.3_spmd, %region_3.4_spmd} | conditional | flops 4724864 | bytes 29720584 | solution.py:164
  134.5 0.1 pad_maximum_fusion.3
  134.5 11.9 %copy.164 = f32[3,8,9216]{1,0,2:T(4,128)} copy(f32[3,8,9216]{2,1,0:T(8,128)S(1)} %pad_maximum_fusion.3) | data formatting | bytes 1769472 | tf_op jit(solution)/shard_map/cond/branch_0_fun/concatenate | solution.py:158
  146.4 0.2 compare_select_fusion.5
  146.7 65.8 %gather_fusion = f32[8192,3,8]{2,1,0:T(4,128)} fusion(f32[3,8,9216]{1,0,2:T(4,128)} %copy.164, s32[8192]{0:T(1024)S(1)} %broadcast_clamp_fusion.5), kind=kCustom, calls=%fused_computation | custom fusion | bytes 1605632 | tf_op jit(solution)/shard_map/cond/branch_0_fun/gather | solution.py:161
  212.5 11.7 %copy.165 = f32[8192,3,8]{0,2,1:T(8,128)S(1)} copy(f32[8192,3,8]{2,1,0:T(4,128)} %gather_fusion) | data formatting | bytes 1572864 | tf_op jit(solution)/shard_map/cond/branch_0_fun/gather | solution.py:161
  224.2 65.8 %gather_fusion.1 = f32[8192,3,8]{2,1,0:T(4,128)} fusion(f32[3,8,9216]{1,0,2:T(4,128)} %copy.164, s32[8192]{0:T(1024)S(1)} %broadcast_clamp_fusion.4), kind=kCustom, calls=%fused_computation.1 | custom fusion | bytes 1605632 | tf_op jit(solution)/shard_map/cond/branch_0_fun/gather | solution.py:161
  290.0 11.7 %copy.167 = f32[8192,3,8]{0,2,1:T(8,128)S(1)} copy(f32[8192,3,8]{2,1,0:T(4,128)} %gather_fusion.1) | data formatting | bytes 1572864 | tf_op jit(solution)/shard_map/cond/branch_0_fun/gather | solution.py:161
  301.7 65.8 %gather_fusion.2 = f32[8192,3,8]{2,1,0:T(4,128)} fusion(f32[3,8,9216]{1,0,2:T(4,128)} %copy.164, s32[8192]{0:T(1024)S(1)} %broadcast_clamp_fusion.3), kind=kCustom, calls=%fused_computation.2 | custom fusion | bytes 1605632 | tf_op jit(solution)/shard_map/cond/branch_0_fun/gather | solution.py:161
  367.5 11.7 %copy.169 = f32[8192,3,8]{0,2,1:T(8,128)S(1)} copy(f32[8192,3,8]{2,1,0:T(4,128)} %gather_fusion.2) | data formatting | bytes 1572864 | tf_op jit(solution)/shard_map/cond/branch_0_fun/gather | solution.py:161
  379.2 65.8 %gather_fusion.3 = f32[8192,3,8]{2,1,0:T(4,128)} fusion(f32[3,8,9216]{1,0,2:T(4,128)} %copy.164, s32[8192]{0:T(1024)S(1)} %broadcast_clamp_fusion.2), kind=kCustom, calls=%fused_computation.3 | custom fusion | bytes 1605632 | tf_op jit(solution)/shard_map/cond/branch_0_fun/gather | solution.py:161
  445.1 12.5 %copy.171 = f32[8192,3,8]{0,2,1:T(8,128)} copy(f32[8192,3,8]{2,1,0:T(4,128)} %gather_fusion.3) | data formatting | bytes 1572864 | tf_op jit(solution)/shard_map/cond/branch_0_fun/gather | solution.py:161
  457.6 65.8 %gather_fusion.4 = f32[8192,3,8]{2,1,0:T(4,128)} fusion(f32[3,8,9216]{1,0,2:T(4,128)} %copy.164, s32[8192]{0:T(1024)S(1)} %broadcast_clamp_fusion.1), kind=kCustom, calls=%fused_computation.4 | custom fusion | bytes 1605632 | tf_op jit(solution)/shard_map/cond/branch_0_fun/gather | solution.py:161
  523.4 12.5 %copy.173 = f32[8192,3,8]{0,2,1:T(8,128)} copy(f32[8192,3,8]{2,1,0:T(4,128)} %gather_fusion.4) | data formatting | bytes 1572864 | tf_op jit(solution)/shard_map/cond/branch_0_fun/gather | solution.py:161
  536.0 65.8 %gather_fusion.5 = f32[8192,3,8]{2,1,0:T(4,128)} fusion(f32[3,8,9216]{1,0,2:T(4,128)} %copy.164, s32[8192]{0:T(1024)S(1)} %broadcast_clamp_fusion), kind=kCustom, calls=%fused_computation.5 | custom fusion | bytes 1605632 | tf_op jit(solution)/shard_map/cond/branch_0_fun/gather | solution.py:161
  601.8 12.5 %copy.175 = f32[8192,3,8]{0,2,1:T(8,128)} copy(f32[8192,3,8]{2,1,0:T(4,128)} %gather_fusion.5) | data formatting | bytes 1572864 | tf_op jit(solution)/shard_map/cond/branch_0_fun/gather | solution.py:161
  614.3 2.8 fusion.21
  617.1 1.2 slice.166
  618.4 9.2 %copy.185 = f32[3,32,1024]{0,2,1:T(8,128)} copy(f32[3,32,1024]{2,0,1:T(4,128)} %all-to-all-done) | data formatting | bytes 786432 | tf_op jit(solution)/shard_map/all_to_all | solution.py:126
  627.6 5.7 constant_dynamic-slice_fusion
  633.3 57.9 %gather_fusion.9 = f32[16384,3]{1,0:T(8,128)} fusion(f32[3,16384]{0,1:T(8,128)} %constant_dynamic-slice_fusion, s32[16384]{0:T(1024)S(1)} %fusion.27), kind=kCustom, calls=%fused_computation.9 | custom fusion | bytes 458752 | tf_op jit(solution)/shard_map/gather | solution.py:129
  691.2 48.0 %multiply_reduce_fusion = f32[3,8192]{0,1:T(8,128)} fusion(f32[3,8192,2]{0,2,1:T(2,128)} %bitcast.118, f32[8192,2]{1,0:T(8,128)} %mul.165), kind=kLoop, calls=%fused_computation.76 | loop fusion | flops 73728 | bytes 360448 | tf_op jit(solution)/shard_map/reduce_sum | solution.py:130
  739.2 2.8 copy.186
  742.0 0.1 copy_add_fusion
  742.2 0.1 copy.187
  742.3 3.0 scatter.4
  (25 shorter events, 0.1 us)
Async XLA Ops:
  61.4 33.1 %copy-start.6 = (s32[2,512]{1,0:T(2,128)S(1)}, s32[2,512]{1,0:T(2,128)}, u32[]{:S(2)}) copy-start(s32[2,512]{1,0:T(2,128)} %param.25) | copy-start | bytes 12292
  61.4 33.1 %copy-start.2 = (f32[2,8192]{1,0:T(2,128)S(1)}, f32[2,8192]{1,0:T(2,128)}, u32[]{:S(2)}) copy-start(f32[2,8192]{1,0:T(2,128)} %param.22) | copy-start | bytes 196612
  61.4 33.1 %copy-start.8 = (f32[8]{0:T(128)S(1)}, f32[8]{0:T(128)}, u32[]{:S(2)}) copy-start(f32[8]{0:T(128)} %param.23) | copy-start | bytes 100
  87.3 531.1 %all-to-all-start = ((f32[3,32,1024]{2,0,1:T(4,128)}), f32[3,32,1024]{2,0,1:T(4,128)}, u32[]{:S(2)}, u32[]{:S(2)}) async-start(f32[3,32,1024]{2,0,1:T(4,128)} %copy.184), calls=%async_computation | async-start | bytes 1048576 | tf_op jit(solution)/shard_map/all_to_all | solution.py:126
  94.5 31.0 %copy-start.3 = (s32[16384]{0:T(1024)S(1)}, s32[16384]{0:T(1024)}, u32[]{:S(2)}) copy-start(s32[16384]{0:T(1024)} %param.19) | copy-start | bytes 196612
  94.5 31.1 %copy-start.1 = (f32[16384]{0:T(1024)S(1)}, f32[16384]{0:T(1024)}, u32[]{:S(2)}) copy-start(f32[16384]{0:T(1024)} %param.20) | copy-start | bytes 196612
  94.5 39.9 %copy-start = (s32[6,8192]{1,0:T(8,128)S(1)}, s32[6,8192]{1,0:T(8,128)}, u32[]{:S(2)}) copy-start(s32[6,8192]{1,0:T(8,128)} %param.24) | copy-start | bytes 589828
  94.5 39.9 %copy-start.4 = (f32[8192]{0:T(1024)S(1)}, f32[8192]{0:T(1024)}, u32[]{:S(2)}) copy-start(f32[8192]{0:T(1024)} %param.26) | copy-start | bytes 98308
  112.6 21.8 %collective-permute-start.1 = (f32[3,8,1,512]{3,1,2,0:T(8,128)S(1)}, f32[3,8,1,512]{3,1,2,0:T(8,128)S(1)}, u32[]{:S(2)}, u32[]{:S(2)}) collective-permute-start(f32[3,8,1,512]{3,1,2,0:T(8,128)S(1)} %copy.179), channel_id=1, source_target_pairs={{1,0},{2,1},{3,2},{4,3},{5,4},{6,5},{7,6},{8,7},{9,8},{10,9},{11,1... | collective-permute-start | bytes 147464 | tf_op jit(solution)/shard_map/ppermute | solution.py:21
  125.5 9.0 %collective-permute-start = (f32[3,8,1,512]{3,1,2,0:T(8,128)S(1)}, f32[3,8,1,512]{3,1,2,0:T(8,128)S(1)}, u32[]{:S(2)}, u32[]{:S(2)}) collective-permute-start(f32[3,8,1,512]{3,1,2,0:T(8,128)S(1)} %copy.177), channel_id=1, source_target_pairs={{0,1},{1,2},{2,3},{3,4},{4,5},{5,6},{6,7},{7,8},{8,9},{9,10},{10,1... | collective-permute-start | bytes 147464 | tf_op jit(solution)/shard_map/ppermute | solution.py:20
  627.6 114.5 %copy-start.7 = (f32[1,3]{1,0:T(1,128)S(1)}, f32[1,3]{1,0:T(1,128)}, u32[]{:S(2)}) copy-start(f32[1,3]{1,0:T(1,128)} %param.21) | copy-start | bytes 40
where the time goes:
time: 748 us; the launch traced here: 745 us
  local copies, waits for them, and re-layouts  661 us (88%)
  other arithmetic  71.5 us (10%)
  starting transfers between devices  12.5 us (2%)
    gather x12, local copies, waits for them, and re-layouts, sweep_ocean(): summed = summed + (extended[:, :, ocean_adjacent[neighbor]] - current)  468 us
    gather x1, local copies, waits for them, and re-layouts, body(): values = incoming[:, intersection_source].reshape(3, -1, INTERSECTIONS)  57.9 us
    gather x1, local copies, waits for them, and re-layouts, body(): outgoing = surface[:, send_rows]  56.6 us
    reduce_sum x2, other arithmetic, body(): regrid = jnp.sum(values * weights, axis=-1) / jnp.sum(weights, axis=-1)  51.3 us
    all_to_all x2, local copies, waits for them, and re-layouts, body(): lax.all_to_all(spread_out, ('sec', 'dom'), split_axis=1, concat_axis=1, t...  19.1 us
    select_n x1, other arithmetic, body(): jnp.where(atmosphere, jnp.concatenate([blank, outgoing], axis=1), jnp.con...  16 us
  transfers between devices with their start and end apart: 3, of which 0 were waited for; matrix products, arithmetic and copies ran while one was open for 70% of the time, Pallas kernels for 0%

commit v1 on v0

v1 whole, which is shorter than its diff:
```python
import functools
import jax
import jax.numpy as jnp
import numpy as np
from jax import lax
from jax.experimental import pallas as pl
from jax.experimental.pallas import tpu as pltpu
from jax.sharding import PartitionSpec as P

TIME_STEP = 0.05
LANES = 128
VMEM = pl.BlockSpec(memory_space=pltpu.VMEM)
SMEM = pl.BlockSpec(memory_space=pltpu.SMEM)
PARAMS = dict(vmem_limit_bytes=48 << 20)


def gll_derivative():
    nodes = np.array([-1.0, -1.0 / np.sqrt(5.0), 1.0 / np.sqrt(5.0), 1.0])
    barycentric = np.array(
        [1.0 / np.prod([nodes[i] - nodes[j] for j in range(4) if j != i]) for i in range(4)]
    )
    matrix = np.zeros((4, 4))
    for i in range(4):
        for j in range(4):
            if i != j:
                matrix[i, j] = barycentric[j] / barycentric[i] / (nodes[i] - nodes[j])
        matrix[i, i] = -np.sum(matrix[i])
    return matrix


DERIVATIVE = gll_derivative()


def two_terms(table):
    high = table.astype(jnp.bfloat16)
    low = (table - high.astype(jnp.float32)).astype(jnp.bfloat16)
    return jnp.concatenate([high, low], axis=1)


def pick(terms, depth, index):
    low = jnp.broadcast_to(index & (LANES - 1), (LANES, index.shape[1]))
    hot = (lax.broadcasted_iota(jnp.int32, low.shape, 0) == low).astype(jnp.float32).astype(jnp.bfloat16)
    found = jnp.dot(terms, jnp.concatenate([hot, hot], axis=0), preferred_element_type=jnp.float32)
    high = jnp.broadcast_to(index >> 7, (depth, index.shape[1]))
    own = lax.broadcasted_iota(jnp.int32, high.shape, 0) == high
    return [
        jnp.sum(jnp.where(own, found[f * depth : (f + 1) * depth], 0.0), axis=0, keepdims=True)
        for f in range(3)
    ]


def send_kernel(surface_ref, rows_ref, out_ref, terms_ref):
    depth = surface_ref.shape[1]
    for f in range(3):
        terms_ref[f * depth : (f + 1) * depth, :] = two_terms(surface_ref[f])
    per_peer = out_ref.shape[2]

    def step(i, _):
        index = jnp.concatenate([rows_ref[pl.ds(2 * i, 1), :], rows_ref[pl.ds(2 * i + 1, 1), :]], axis=1)
        values = pick(terms_ref[...], depth, index)
        for k in range(2):
            place = 2 * i + k
            for f in range(3):
                out_ref[place // per_peer, f, pl.ds(place % per_peer, 1), :] = values[f][
                    :, k * LANES : (k + 1) * LANES
                ]
        return 0

    lax.fori_loop(0, rows_ref.shape[0] // 2, step, 0)


def exchange_kernel(n, out_ref, in_ref, send_sem, recv_sem):
    sec, dom = lax.axis_index("sec"), lax.axis_index("dom")
    barrier = pltpu.get_barrier_semaphore()

    def greet(p, _):
        pl.semaphore_signal(barrier, inc=1, device_id=(1 - sec, p), device_id_type=pl.DeviceIdType.MESH)
        return 0

    lax.fori_loop(0, n, greet, 0)
    pl.semaphore_wait(barrier, n)

    def copy(k):
        p = lax.rem(dom + k, n)
        return pltpu.make_async_remote_copy(
            src_ref=out_ref.at[p],
            dst_ref=in_ref.at[dom],
            send_sem=send_sem.at[k],
            recv_sem=recv_sem.at[k],
            device_id=(1 - sec, p),
            device_id_type=pl.DeviceIdType.MESH,
        )

    def start(k, _):
        copy(k).start()
        return 0

    def wait(k, _):
        copy(k).wait()
        return 0

    lax.fori_loop(0, n, start, 0)
    lax.fori_loop(0, n, wait, 0)


def lane_phase(shape):
    return lax.broadcasted_iota(jnp.int32, shape, 1) % 4


def along_second(value, phase):
    width = value.shape[1]
    total = jnp.zeros_like(value)
    for shift in range(-3, 4):
        factor = jnp.zeros(value.shape, jnp.float32)
        for i in range(4):
            if 0 <= i + shift < 4:
                factor = jnp.where(phase == i, np.float32(DERIVATIVE[i, i + shift]), factor)
        moved = value if shift == 0 else pltpu.roll(value, (-shift) % width, 1)
        total = total + factor * moved
    return total


def advance_kernel(x_points, y_points, state_ref, metric_ref, speed_ref, stepped_ref):
    @pl.when(lax.axis_index("sec") == 0)
    def _():
        def piece(g, _):
            def at(i, f):
                return state_ref[f, :, pl.ds(pl.multiple_of(start + i * y_points, LANES), LANES)]

            start = (g // (y_points // LANES)) * 4 * y_points + (g % (y_points // LANES)) * LANES
            phase = lane_phase((state_ref.shape[1], LANES))
            u = [at(i, 0) for i in range(4)]
            v = [at(i, 1) for i in range(4)]
            h = [at(i, 2) for i in range(4)]
            speed = speed_ref[...]
            for i in range(4):
                here = pl.ds(pl.multiple_of(start + i * y_points, LANES), LANES)
                gx = metric_ref[0:1, here]
                gy = metric_ref[1:2, here]
                dx_h = sum(np.float32(DERIVATIVE[i, j]) * h[j] for j in range(4))
                dx_u = sum(np.float32(DERIVATIVE[i, j]) * u[j] for j in range(4))
                stepped_ref[0, :, here] = u[i] - TIME_STEP * (gx * dx_h)
                stepped_ref[1, :, here] = v[i] - TIME_STEP * (gy * along_second(h[i], phase))
                spread = gx * dx_u + gy * along_second(v[i], phase)
                stepped_ref[2, :, here] = h[i] - TIME_STEP * speed * spread
            return 0

        lax.fori_loop(0, x_points // 4 * (y_points // LANES), piece, 0)

    @pl.when(lax.axis_index("sec") == 1)
    def _():
        for f in range(3):
            stepped_ref[f] = state_ref[f]


def to_rows(source_ref, source_at, table_ref, table_at, count):
    def piece(c, _):
        here = pl.ds(pl.multiple_of(source_at + c * LANES, LANES), LANES)
        block = jnp.concatenate([source_ref[f, :, here] for f in range(3)], axis=0)
        fill = jnp.zeros((LANES - block.shape[0], LANES), jnp.float32)
        table_ref[pl.ds(pl.multiple_of(table_at + c * LANES, LANES), LANES), :] = jnp.transpose(
            jnp.concatenate([block, fill], axis=0)
        )
        return 0

    lax.fori_loop(0, count // LANES, piece, 0)


def from_rows(table_ref, at, levels):
    block = jnp.transpose(table_ref[pl.ds(pl.multiple_of(at, LANES), LANES), :])
    return [block[f * levels : (f + 1) * levels] for f in range(3)]


def edge_kernel(state_ref, edges_ref, border_ref, table_ref, picked_ref):
    rows = state_ref.shape[2]
    count = edges_ref.shape[0]
    to_rows(state_ref, 0, table_ref, 0, rows)

    def step(i, _):
        base = i * 16
        places = [edges_ref[base + u] for u in range(16)]
        for u in range(16):
            picked_ref[pl.ds(base + u, 1), :] = table_ref[pl.ds(places[u], 1), :]
        return 0

    lax.fori_loop(0, count // 16, step, 0)
    for c in range(count // LANES):
        block = from_rows(picked_ref, c * LANES, state_ref.shape[1])
        for f in range(3):
            border_ref[f, :, c * LANES : (c + 1) * LANES] = block[f]


def sweep_kernel(state_ref, west_ref, east_ref, adjacent_ref, kappa_ref, swept_ref, table_ref, sum_ref):
    levels, rows, edge = state_ref.shape[1], state_ref.shape[2], west_ref.shape[2]
    part = swept_ref.shape[2]
    to_rows(state_ref, 0, table_ref, 0, rows)
    to_rows(west_ref, 0, table_ref, rows, edge)
    to_rows(east_ref, 0, table_ref, rows + edge, edge)

    def step(i, _):
        base = i * 16
        places = [[adjacent_ref[base + (j * part + u)] for j in range(6)] for u in range(16)]
        for u in range(16):
            a = [table_ref[pl.ds(p, 1), :] for p in places[u]]
            sum_ref[pl.ds(base + u, 1), :] = ((a[0] + a[1]) + (a[2] + a[3])) + (a[4] + a[5])
        return 0

    lax.fori_loop(0, part // 16, step, 0)
    first = lax.axis_index("sec") * part

    def finish(c, _):
        here = pl.ds(pl.multiple_of(c * LANES, LANES), LANES)
        there = pl.ds(pl.multiple_of(first + c * LANES, LANES), LANES)
        block = from_rows(sum_ref, c * LANES, levels)
        kappa = kappa_ref[0:1, here]
        for f in range(3):
            value = state_ref[f, :, there]
            swept_ref[f, :, here] = value + kappa * (block[f] - 6.0 * value)
        return 0

    lax.fori_loop(0, part // LANES, finish, 0)


def deinterleave(values, offset):
    count = values.shape[0]
    i = lax.broadcasted_iota(jnp.int32, (LANES, LANES), 0)
    j = lax.broadcasted_iota(jnp.int32, (LANES, LANES), 1)
    m = lax.broadcasted_iota(jnp.int32, (count // 2, count), 0)
    q = lax.broadcasted_iota(jnp.int32, (count // 2, count), 1)
    total = jnp.zeros((count // 2, LANES), jnp.float32)
    for b in range(2):
        chosen = (i == 2 * (j - b * (LANES // 2)) + offset).astype(jnp.float32)
        packed = jnp.dot(
            values, chosen, preferred_element_type=jnp.float32, precision=lax.Precision.HIGHEST
        )
        gathered = (q == 2 * m + b).astype(jnp.float32)
        total = total + jnp.dot(
            gathered, packed, preferred_element_type=jnp.float32, precision=lax.Precision.HIGHEST
        )
    return total


def final_kernel(
    x_points, y_points, incoming_ref, source_ref, weight_ref, rate_ref, stepped_ref, west_ref, east_ref,
    own_ref, helped_ref, new_ref, terms_ref, index_ref, share_ref,
):
    atmosphere = lax.axis_index("sec") == 0
    levels = stepped_ref.shape[1]
    depth = source_ref.shape[0]

    @pl.when(atmosphere)
    def _():
        for f in range(3):
            for x in range(x_points):
                here = slice(x * y_points, (x + 1) * y_points)
                value = stepped_ref[f, :, here]
                if x % 4 == 3:
                    other = (
                        stepped_ref[f, :, (x + 1) * y_points : (x + 2) * y_points]
                        if x < x_points - 1
                        else east_ref[f]
                    )
                    value = (value + other) * 0.5
                elif x % 4 == 0:
                    other = stepped_ref[f, :, (x - 1) * y_points : x * y_points] if x else west_ref[f]
                    value = (value + other) * 0.5
                position = lax.broadcasted_iota(jnp.int32, value.shape, 1)
                phase = position % 4
                after = pltpu.roll(value, y_points - 1, 1)
                before = pltpu.roll(value, 1, 1)
                new_ref[f, :, here] = jnp.where(
                    (phase == 3) & (position < y_points - 1),
                    (value + after) * 0.5,
                    jnp.where((phase == 0) & (position > 0), (value + before) * 0.5, value),
                )

    @pl.when(jnp.logical_not(atmosphere))
    def _():
        part = own_ref.shape[2]
        for f in range(3):
            new_ref[f, :, :part] = helped_ref[f]
            new_ref[f, :, part:] = own_ref[f]

    for f in range(3):
        table = incoming_ref[:, f].reshape(depth, LANES)
        terms_ref[f * depth : (f + 1) * depth, :] = two_terms(table)
    source = source_ref[...].astype(jnp.float32)
    for k in range(2):
        index_ref[:, k * LANES : (k + 1) * LANES] = (deinterleave(source, k) + 0.5).astype(jnp.int32)
        share_ref[:, k * LANES : (k + 1) * LANES] = deinterleave(weight_ref[...], k)

    def step(c, _):
        values = pick(terms_ref[...], depth, index_ref[pl.ds(c, 1), :])
        weight = share_ref[pl.ds(c, 1), :]
        whole = weight[:, :LANES] + weight[:, LANES:]
        here = pl.ds(pl.multiple_of(c * LANES, LANES), LANES)
        for f in range(3):
            product = values[f] * weight
            regrid = (product[:, :LANES] + product[:, LANES:]) / whole
            top = new_ref[f, levels - 1 : levels, here]
            new_ref[f, levels - 1 : levels, here] = top + rate_ref[0, f] * (regrid - top)
        return 0

    lax.fori_loop(0, depth // 2, step, 0)


def body(
    state, send_rows, intersection_source, intersection_weight, couple_rate, atm_metric, wave_speed,
    ocean_adjacent, ocean_edges, ocean_kappa,
):
    levels, rows = state.shape[1], state.shape[2]
    y_points = ocean_edges.shape[1]
    x_points = rows // y_points
    n = lax.axis_size("dom")
    sec = lax.axis_index("sec")
    slots = send_rows.shape[0]
    cap = slots // n
    part = rows // 2
    f32 = jnp.float32

    ocean = lax.ppermute(state, "sec", [(1, 0)])
    ocean = jnp.where(sec == 0, ocean, state)

    surface = state[:, levels - 1].reshape(3, rows // LANES, LANES)
    outgoing = pl.pallas_call(
        send_kernel,
        out_shape=jax.ShapeDtypeStruct((n, 3, cap // LANES, LANES), f32),
        in_specs=[VMEM] * 2,
        out_specs=VMEM,
        scratch_shapes=[pltpu.VMEM((3 * rows // LANES, 2 * LANES), jnp.bfloat16)],
        compiler_params=pltpu.CompilerParams(**PARAMS),
        name="pick_sent",
    )(surface, send_rows.reshape(-1, LANES))
    incoming = pl.pallas_call(
        functools.partial(exchange_kernel, n),
        out_shape=jax.ShapeDtypeStruct(outgoing.shape, f32),
        in_specs=[VMEM],
        out_specs=VMEM,
        scratch_shapes=[
            pltpu.SemaphoreType.DMA((n,)),
            pltpu.SemaphoreType.DMA((n,)),
        ],
        compiler_params=pltpu.CompilerParams(collective_id=0, has_side_effects=True, **PARAMS),
        name="exchange",
    )(outgoing)

    stepped = pl.pallas_call(
        functools.partial(advance_kernel, x_points, y_points),
        out_shape=jax.ShapeDtypeStruct(state.shape, f32),
        in_specs=[VMEM] * 3,
        out_specs=VMEM,
        compiler_params=pltpu.CompilerParams(**PARAMS),
        name="advance",
    )(state, atm_metric, jnp.broadcast_to(wave_speed[:, None], (levels, LANES)))
    rim = pl.pallas_call(
        edge_kernel,
        out_shape=jax.ShapeDtypeStruct((3, levels, 2 * y_points), f32),
        in_specs=[VMEM, SMEM],
        out_specs=VMEM,
        scratch_shapes=[pltpu.VMEM((rows, LANES), f32), pltpu.VMEM((2 * y_points, LANES), f32)],
        compiler_params=pltpu.CompilerParams(**PARAMS),
        name="pick_edges",
    )(ocean, ocean_edges.reshape(-1))

    up = [(i, (i + 1) % n) for i in range(n)]
    down = [(j, i) for i, j in up]
    eastward = jnp.stack([stepped[:, :, rows - y_points :], rim[:, :, y_points:]])
    westward = jnp.stack([stepped[:, :, :y_points], rim[:, :, :y_points]])
    west = lax.ppermute(eastward, "dom", up)
    east = lax.ppermute(westward, "dom", down)

    adjacent = lax.dynamic_slice_in_dim(ocean_adjacent, sec * part, part, 1).reshape(-1)
    kappa = lax.dynamic_slice_in_dim(ocean_kappa, sec * part, part, 0).reshape(1, -1)
    swept = pl.pallas_call(
        sweep_kernel,
        out_shape=jax.ShapeDtypeStruct((3, levels, part), f32),
        in_specs=[VMEM] * 3 + [SMEM, VMEM],
        out_specs=VMEM,
        scratch_shapes=[
            pltpu.VMEM((rows + 2 * y_points, LANES), f32),
            pltpu.VMEM((part, LANES), f32),
        ],
        compiler_params=pltpu.CompilerParams(**PARAMS),
        name="sweep",
    )(ocean, west[1], east[1], adjacent, kappa)
    helped = lax.ppermute(swept, "sec", [(0, 1)])

    return pl.pallas_call(
        functools.partial(final_kernel, x_points, y_points),
        out_shape=jax.ShapeDtypeStruct(state.shape, f32),
        in_specs=[VMEM] * 3 + [SMEM] + [VMEM] * 5,
        out_specs=VMEM,
        scratch_shapes=[
            pltpu.VMEM((3 * slots // LANES, 2 * LANES), jnp.bfloat16),
            pltpu.VMEM((slots // LANES // 2, 2 * LANES), jnp.int32),
            pltpu.VMEM((slots // LANES // 2, 2 * LANES), f32),
        ],
        compiler_params=pltpu.CompilerParams(**PARAMS),
        name="finish",
    )(
        incoming,
        intersection_source.reshape(-1, LANES),
        intersection_weight.reshape(-1, LANES),
        couple_rate,
        stepped,
        west[0],
        east[0],
        swept,
        helped,
    )


def solution(mesh):
    in_specs = (
        P(None, None, ("sec", "dom")),
        P(("sec", "dom")),
        P(("sec", "dom")),
        P(("sec", "dom")),
        P("sec", None),
        P(None, "dom"),
        P(),
        P(None, "dom"),
        P(None, "dom"),
        P("dom"),
    )
    out_specs = P(None, None, ("sec", "dom"))
    return jax.shard_map(body, mesh=mesh, in_specs=in_specs, out_specs=out_specs, check_vma=False)
```

time: 748 us -> 104 us (0.14)
  the two profiles are of different devices: /device:TPU:1 before, /device:TPU:0 now
where the time goes in v1:
time: 104 us
  Pallas kernels  81.7 us (79%)
  starting transfers between devices  9.91 us (10%)
  waiting for transfers between devices  8.2 us (8%)
  local copies, waits for them, and re-layouts  4.07 us (4%)
    pallas_call x1, Pallas kernels, body(): pl.pallas_call(sweep_kernel, out_shape=jax.ShapeDtypeStruct((3, levels, p...  32.8 us
    pallas_call x1, Pallas kernels, body(): pl.pallas_call(functools.partial(final_kernel, x_points, y_points), out_s...  18.7 us
    pallas_call x1, Pallas kernels, body(): pl.pallas_call(send_kernel, out_shape=jax.ShapeDtypeStruct((n, 3, cap //...  12.5 us
    pallas_call x1, Pallas kernels, body(): pl.pallas_call(edge_kernel, out_shape=jax.ShapeDtypeStruct((3, levels, 2...  8.24 us
    pallas_call x1, Pallas kernels, body(): pl.pallas_call(functools.partial(exchange_kernel, n), out_shape=jax.Shape...  7.41 us
    ppermute x1, starting transfers between devices, body(): east = lax.ppermute(westward, 'dom', down)  6.98 us
    ppermute x1, waiting for transfers between devices, body(): west = lax.ppermute(eastward, 'dom', up)  6.05 us
    unnamed x21, local copies, waits for them, and re-layouts  3.81 us
  transfers between devices with their start and end apart: 4, of which 2 were waited for; matrix products, arithmetic and copies ran while one was open for 0% of the time, Pallas kernels for 21%

profile of v1, /device:TPU:0, one launch (start us, length us, event | category | flops | bytes accessed | tf_op | source)
XLA Modules:
  0.0 104.2 jit_solution(4329334392437350561)
XLA Ops:
  0.0 0.0 copy-start
  0.0 1.4 %collective-permute-start = (f32[3,8,8192]{2,1,0:T(8,128)}, f32[3,8,8192]{2,1,0:T(8,128)S(1)}, u32[]{:S(2)}, u32[]{:S(2)}) collective-permute-start(f32[3,8,8192]{2,1,0:T(8,128)} %state_ref.1), channel_id=1, source_target_pairs={{16,0},{17,1},{18,2},{19,3},{20,4},{21,5},{22,6},{23,7},{24,8},{25... | collective-permute-start | bytes 2359304 | tf_op jit(solution)/shard_map/ppermute | solution.py:321
  1.4 0.0 copy-done
  1.5 0.0 copy-start.7
  1.5 0.0 copy-start.2
  1.5 0.1 reshape.23.adjacent_ref
  1.5 0.7 copy-done.7
  2.2 0.0 copy-start.8
  2.2 0.7 copy-done.8
  2.9 0.0 copy-start.9
  2.9 0.7 copy-done.9
  3.6 0.1 broadcast_in_dim.2.speed_ref
  3.6 0.0 copy-done.2
  3.6 0.0 copy-start.1
  3.6 1.1 %copy-done.1 = f32[3,8,8192]{2,1,0:T(8,128)S(1)} copy-done((f32[3,8,8192]{2,1,0:T(8,128)S(1)}, f32[3,8,8192]{2,1,0:T(8,128)}, u32[]{:S(2)}) %copy-start.1) | copy-done | bytes 786456
  4.8 2.0 %advance.1.stepped_ref = f32[3,8,8192]{2,1,0:T(8,128)S(1)} custom-call(f32[3,8,8192]{2,1,0:T(8,128)S(1)} %copy-done.1, f32[2,8192]{1,0:T(2,128)S(1)} %copy-done.2, f32[8,128]{1,0:T(8,128)S(1)} %broadcast_in_dim.2.speed_ref), custom_call_target="tpu_custom_call" | custom-call | tf_op jit(solution)/shard_map/advance/pallas_call | solution.py:347
  6.8 0.0 collective-permute-done
  6.8 0.1 broadcast_select_fusion.state_ref
  6.9 8.2 %pick_edges.1 = f32[3,8,1024]{2,1,0:T(8,128)S(1)} custom-call(f32[3,8,8192]{2,1,0:T(8,128)S(1)} %broadcast_select_fusion.state_ref, s32[1024]{0:T(1024)S(1)} %bitcast.28), custom_call_target="tpu_custom_call" | custom-call | tf_op jit(solution)/shard_map/pick_edges/pallas_call | solution.py:355
  15.2 7.0 %collective-permute-start.2 = (f32[2,3,8,512]{3,2,1,0:T(8,128)S(1)}, f32[2,3,8,512]{3,2,1,0:T(8,128)S(1)}, u32[]{:S(2)}, u32[]{:S(2)}) collective-permute-start(f32[2,3,8,512]{3,2,1,0:T(8,128)S(1)} %pad_maximum_fusion.1), channel_id=1, source_target_pairs={{1,0},{2,1},{3,2},{4,3},{5,4},{6,5},{7,6},{8,7},{9,8},{10,9},{11,1... | collective-permute-start | bytes 294920 | tf_op jit(solution)/shard_map/ppermute | solution.py:370
  22.2 0.1 collective-permute-start.1
  22.3 2.1 %collective-permute-done.2 = f32[2,3,8,512]{3,2,1,0:T(8,128)S(1)} collective-permute-done((f32[2,3,8,512]{3,2,1,0:T(8,128)S(1)}, f32[2,3,8,512]{3,2,1,0:T(8,128)S(1)}, u32[]{:S(2)}, u32[]{:S(2)}) %collective-permute-start.2) | collective-permute-done | bytes 98336 | tf_op jit(solution)/shard_map/ppermute | solution.py:370
  24.4 6.0 %collective-permute-done.1 = f32[2,3,8,512]{3,2,1,0:T(8,128)S(1)} collective-permute-done((f32[2,3,8,512]{3,2,1,0:T(8,128)S(1)}, f32[2,3,8,512]{3,2,1,0:T(8,128)S(1)}, u32[]{:S(2)}, u32[]{:S(2)}) %collective-permute-start.1) | collective-permute-done | bytes 98336 | tf_op jit(solution)/shard_map/ppermute | solution.py:369
  30.5 32.8 %sweep.1.own_ref = f32[3,8,4096]{2,1,0:T(8,128)S(1)} custom-call(f32[3,8,8192]{2,1,0:T(8,128)S(1)} %broadcast_select_fusion.state_ref, f32[3,8,512]{2,1,0:T(8,128)S(1)} %get-tuple-element.9.west_ref, f32[3,8,512]{2,1,0:T(8,128)S(1)} %get-tuple-element.7.east_ref, s32[24576]{0:T(1024)S(1)} %reshape.23.adjacent_ref, f32[1,4096]{1,0:T(1,128)S(1)} %bitcast.24), custom_call_target="tpu_custom_call" | custom-call | tf_op jit(solution)/shard_map/sweep/pallas_call | solution.py:374
  63.3 0.0 copy-start.5
  63.3 1.5 %collective-permute-start.3 = (f32[3,8,4096]{2,1,0:T(8,128)S(1)}, f32[3,8,4096]{2,1,0:T(8,128)S(1)}, u32[]{:S(2)}, u32[]{:S(2)}) collective-permute-start(f32[3,8,4096]{2,1,0:T(8,128)S(1)} %sweep.1.own_ref), channel_id=1, source_target_pairs={{0,16},{1,17},{2,18},{3,19},{4,20},{5,21},{6,22},{7,23},{8,24},{9,... | collective-permute-start | bytes 1179656 | tf_op jit(solution)/shard_map/ppermute | solution.py:386
  64.7 0.1 slice.27
  64.8 0.0 copy-done.5
  64.8 12.5 %pick_sent.1.out_ref = f32[16,3,8,128]{3,2,1,0:T(8,128)S(1)} custom-call(f32[3,64,128]{2,1,0:T(8,128)S(1)} %bitcast.23, s32[128,128]{1,0:T(8,128)S(1)} %bitcast.27), custom_call_target="tpu_custom_call" | custom-call | tf_op jit(solution)/shard_map/pick_sent/pallas_call | solution.py:325
  77.4 0.0 copy-start.3
  77.4 0.0 copy-start.4
  77.4 7.4 %exchange.1.incoming_ref = f32[16,3,8,128]{3,2,1,0:T(8,128)S(1)} custom-call(f32[16,3,8,128]{3,2,1,0:T(8,128)S(1)} %pick_sent.1.out_ref), custom_call_target="tpu_custom_call" | custom-call | tf_op jit(solution)/shard_map/exchange/pallas_call | solution.py:334
  84.8 0.0 collective-permute-done.3.helped_ref
  84.8 0.0 copy-start.6
  84.8 0.0 copy-done.3
  84.9 0.0 copy-done.4
  84.9 0.6 copy-done.6
  85.5 18.7 %finish.1 = f32[3,8,8192]{2,1,0:T(8,128)} custom-call(f32[16,3,8,128]{3,2,1,0:T(8,128)S(1)} %exchange.1.incoming_ref, s32[128,128]{1,0:T(8,128)S(1)} %bitcast.25, f32[128,128]{1,0:T(8,128)S(1)} %bitcast.26, f32[1,3]{1,0:T(1,128)S(1)} %copy-done.6, f32[3,8,8192]{2,1,0:T(8,128)S(1)} %advance.1.stepped_ref, f32[3,8,512]{2,1,0:T(8,128)S(1)} %get-tuple-element.10.west_ref, ...), custom_call_target="tpu_custom_call" | custom-call | tf_op jit(solution)/shard_map/finish/pallas_call | solution.py:388
  (9 shorter events, 0.1 us)
Async XLA Ops:
  0.0 1.4 %copy-start = (s32[6,8192]{1,0:T(8,128)S(1)}, s32[6,8192]{1,0:T(8,128)}, u32[]{:S(2)}) copy-start(s32[6,8192]{1,0:T(8,128)} %param.17) | copy-start | bytes 589828
  0.0 6.8 %collective-permute-start = (f32[3,8,8192]{2,1,0:T(8,128)}, f32[3,8,8192]{2,1,0:T(8,128)S(1)}, u32[]{:S(2)}, u32[]{:S(2)}) collective-permute-start(f32[3,8,8192]{2,1,0:T(8,128)} %state_ref.1), channel_id=1, source_target_pairs={{16,0},{17,1},{18,2},{19,3},{20,4},{21,5},{22,6},{23,7},{24,8},{25... | collective-permute-start | bytes 2359304 | tf_op jit(solution)/shard_map/ppermute | solution.py:321
  1.5 0.8 copy-start.7
  1.5 2.2 %copy-start.2 = (f32[2,8192]{1,0:T(2,128)S(1)}, f32[2,8192]{1,0:T(2,128)}, u32[]{:S(2)}) copy-start(f32[2,8192]{1,0:T(2,128)} %metric_ref.1) | copy-start | bytes 196612
  2.2 0.7 copy-start.8
  2.9 0.7 copy-start.9
  3.6 1.1 %copy-start.1 = (f32[3,8,8192]{2,1,0:T(8,128)S(1)}, f32[3,8,8192]{2,1,0:T(8,128)}, u32[]{:S(2)}) copy-start(f32[3,8,8192]{2,1,0:T(8,128)} %state_ref.1) | copy-start | bytes 2359300
  15.2 9.2 %collective-permute-start.2 = (f32[2,3,8,512]{3,2,1,0:T(8,128)S(1)}, f32[2,3,8,512]{3,2,1,0:T(8,128)S(1)}, u32[]{:S(2)}, u32[]{:S(2)}) collective-permute-start(f32[2,3,8,512]{3,2,1,0:T(8,128)S(1)} %pad_maximum_fusion.1), channel_id=1, source_target_pairs={{1,0},{2,1},{3,2},{4,3},{5,4},{6,5},{7,6},{8,7},{9,8},{10,9},{11,1... | collective-permute-start | bytes 294920 | tf_op jit(solution)/shard_map/ppermute | solution.py:370
  22.2 8.3 %collective-permute-start.1 = (f32[2,3,8,512]{3,2,1,0:T(8,128)S(1)}, f32[2,3,8,512]{3,2,1,0:T(8,128)S(1)}, u32[]{:S(2)}, u32[]{:S(2)}) collective-permute-start(f32[2,3,8,512]{3,2,1,0:T(8,128)S(1)} %pad_maximum_fusion), channel_id=1, source_target_pairs={{0,1},{1,2},{2,3},{3,4},{4,5},{5,6},{6,7},{7,8},{8,9},{9,10},{10,1... | collective-permute-start | bytes 294920 | tf_op jit(solution)/shard_map/ppermute | solution.py:369
  63.3 1.6 %copy-start.5 = (s32[16384]{0:T(1024)S(1)}, s32[16384]{0:T(1024)}, u32[]{:S(2)}) copy-start(s32[16384]{0:T(1024)} %param.11) | copy-start | bytes 196612
  63.3 21.6 %collective-permute-start.3 = (f32[3,8,4096]{2,1,0:T(8,128)S(1)}, f32[3,8,4096]{2,1,0:T(8,128)S(1)}, u32[]{:S(2)}, u32[]{:S(2)}) collective-permute-start(f32[3,8,4096]{2,1,0:T(8,128)S(1)} %sweep.1.own_ref), channel_id=1, source_target_pairs={{0,16},{1,17},{2,18},{3,19},{4,20},{5,21},{6,22},{7,23},{8,24},{9,... | collective-permute-start | bytes 1179656 | tf_op jit(solution)/shard_map/ppermute | solution.py:386
  77.4 7.5 %copy-start.3 = (s32[16384]{0:T(1024)S(1)}, s32[16384]{0:T(1024)}, u32[]{:S(2)}) copy-start(s32[16384]{0:T(1024)} %param.12) | copy-start | bytes 196612
  77.4 7.5 %copy-start.4 = (f32[16384]{0:T(1024)S(1)}, f32[16384]{0:T(1024)}, u32[]{:S(2)}) copy-start(f32[16384]{0:T(1024)} %param.13) | copy-start | bytes 196612
  84.8 0.7 copy-start.6

commit v2 on v1

--- a/solution.py
+++ b/solution.py
@@ -66,19 +66,48 @@
                 ]
         return 0
 
-    lax.fori_loop(0, rows_ref.shape[0] // 2, step, 0)
-
-
-def exchange_kernel(n, out_ref, in_ref, send_sem, recv_sem):
+    lax.fori_loop(0, rows_ref.shape[0] // 2, step, 0, unroll=4)
+
+
+def exchange_kernel(
+    n, out_ref, stepped_ref, rim_ref, in_ref, west_a_ref, east_a_ref, west_o_ref, east_o_ref,
+    send_sem, recv_sem, edge_send_sem, edge_recv_sem,
+):
     sec, dom = lax.axis_index("sec"), lax.axis_index("dom")
+    right, left = lax.rem(dom + 1, n), lax.rem(dom + n - 1, n)
+    mesh_ids = pl.DeviceIdType.MESH
     barrier = pltpu.get_barrier_semaphore()
 
     def greet(p, _):
-        pl.semaphore_signal(barrier, inc=1, device_id=(1 - sec, p), device_id_type=pl.DeviceIdType.MESH)
+        pl.semaphore_signal(barrier, inc=1, device_id=(1 - sec, p), device_id_type=mesh_ids)
         return 0
 
     lax.fori_loop(0, n, greet, 0)
-    pl.semaphore_wait(barrier, n)
+    for side in (left, right):
+        pl.semaphore_signal(barrier, inc=1, device_id=(sec, side), device_id_type=mesh_ids)
+    pl.semaphore_wait(barrier, n + 2)
+
+    edge, rows = west_a_ref.shape[2], stepped_ref.shape[2]
+    first, last = pl.ds(0, edge), pl.ds(rows - edge, edge)
+    edges = []
+    for k, (source, target, side) in enumerate(
+        (
+            (rim_ref.at[:, :, pl.ds(edge, edge)], west_o_ref, right),
+            (rim_ref.at[:, :, first], east_o_ref, left),
+            (stepped_ref.at[:, :, last], west_a_ref, right),
+            (stepped_ref.at[:, :, first], east_a_ref, left),
+        )
+    ):
+        edges.append(
+            pltpu.make_async_remote_copy(
+                src_ref=source,
+                dst_ref=target,
+                send_sem=edge_send_sem.at[k],
+                recv_sem=edge_recv_sem.at[k],
+                device_id=(sec, side),
+                device_id_type=mesh_ids,
+            )
+        )
 
     def copy(k):
         p = lax.rem(dom + k, n)
@@ -88,7 +117,7 @@
             send_sem=send_sem.at[k],
             recv_sem=recv_sem.at[k],
             device_id=(1 - sec, p),
-            device_id_type=pl.DeviceIdType.MESH,
+            device_id_type=mesh_ids,
         )
 
     def start(k, _):
@@ -99,8 +128,12 @@
         copy(k).wait()
         return 0
 
+    for each in edges:
+        each.start()
     lax.fori_loop(0, n, start, 0)
     lax.fori_loop(0, n, wait, 0)
+    for each in edges:
+        each.wait()
 
 
 def lane_phase(shape):
@@ -157,13 +190,11 @@
     def piece(c, _):
         here = pl.ds(pl.multiple_of(source_at + c * LANES, LANES), LANES)
         block = jnp.concatenate([source_ref[f, :, here] for f in range(3)], axis=0)
-        fill = jnp.zeros((LANES - block.shape[0], LANES), jnp.float32)
-        table_ref[pl.ds(pl.multiple_of(table_at + c * LANES, LANES), LANES), :] = jnp.transpose(
-            jnp.concatenate([block, fill], axis=0)
-        )
-        return 0
-
-    lax.fori_loop(0, count // LANES, piece, 0)
+        there = pl.ds(pl.multiple_of(table_at + c * LANES, LANES), LANES)
+        table_ref[there, : block.shape[0]] = jnp.transpose(block)
+        return 0
+
+    lax.fori_loop(0, count // LANES, piece, 0, unroll=4)
 
 
 def from_rows(table_ref, at, levels):
@@ -218,7 +249,7 @@
             swept_ref[f, :, here] = value + kappa * (block[f] - 6.0 * value)
         return 0
 
-    lax.fori_loop(0, part // LANES, finish, 0)
+    lax.fori_loop(0, part // LANES, finish, 0, unroll=4)
 
 
 def deinterleave(values, offset):
@@ -240,13 +271,40 @@
     return total
 
 
-def final_kernel(
-    x_points, y_points, incoming_ref, source_ref, weight_ref, rate_ref, stepped_ref, west_ref, east_ref,
-    own_ref, helped_ref, new_ref, terms_ref, index_ref, share_ref,
+def regrid_kernel(incoming_ref, source_ref, weight_ref, regrid_ref, terms_ref, index_ref, share_ref):
+    depth = source_ref.shape[0]
+    for f in range(3):
+        table = incoming_ref[:, f].reshape(depth, LANES)
+        terms_ref[f * depth : (f + 1) * depth, :] = two_terms(table)
+    source = source_ref[...].astype(jnp.float32)
+    for k in range(2):
+        index_ref[:, k * LANES : (k + 1) * LANES] = (deinterleave(source, k) + 0.5).astype(jnp.int32)
+        share_ref[:, k * LANES : (k + 1) * LANES] = deinterleave(weight_ref[...], k)
+
+    def step(c, _):
+        values = pick(terms_ref[...], depth, index_ref[pl.ds(c, 1), :])
+        weight = share_ref[pl.ds(c, 1), :]
+        whole = weight[:, :LANES] + weight[:, LANES:]
+        here = pl.ds(pl.multiple_of(c * LANES, LANES), LANES)
+        for f in range(3):
+            product = values[f] * weight
+            regrid_ref[f : f + 1, here] = (product[:, :LANES] + product[:, LANES:]) / whole
+        return 0
+
+    lax.fori_loop(0, depth // 2, step, 0, unroll=4)
+
+
+def finish_kernel(
+    x_points, y_points, regrid_ref, rate_ref, stepped_ref, west_ref, east_ref, own_ref, helped_ref, new_ref,
 ):
     atmosphere = lax.axis_index("sec") == 0
     levels = stepped_ref.shape[1]
-    depth = source_ref.shape[0]
+
+    def couple(f, here, value):
+        rate = rate_ref[0, f]
+        row = lax.broadcasted_iota(jnp.int32, value.shape, 0)
+        relaxed = value + rate * (regrid_ref[f : f + 1, here] - value)
+        new_ref[f, :, here] = jnp.where(row == levels - 1, relaxed, value)
 
     @pl.when(atmosphere)
     def _():
@@ -268,40 +326,19 @@
                 phase = position % 4
                 after = pltpu.roll(value, y_points - 1, 1)
                 before = pltpu.roll(value, 1, 1)
-                new_ref[f, :, here] = jnp.where(
+                averaged = jnp.where(
                     (phase == 3) & (position < y_points - 1),
                     (value + after) * 0.5,
                     jnp.where((phase == 0) & (position > 0), (value + before) * 0.5, value),
                 )
+                couple(f, here, averaged)
 
     @pl.when(jnp.logical_not(atmosphere))
     def _():
         part = own_ref.shape[2]
         for f in range(3):
-            new_ref[f, :, :part] = helped_ref[f]
-            new_ref[f, :, part:] = own_ref[f]
-
-    for f in range(3):
-        table = incoming_ref[:, f].reshape(depth, LANES)
-        terms_ref[f * depth : (f + 1) * depth, :] = two_terms(table)
-    source = source_ref[...].astype(jnp.float32)
-    for k in range(2):
-        index_ref[:, k * LANES : (k + 1) * LANES] = (deinterleave(source, k) + 0.5).astype(jnp.int32)
-        share_ref[:, k * LANES : (k + 1) * LANES] = deinterleave(weight_ref[...], k)
-
-    def step(c, _):
-        values = pick(terms_ref[...], depth, index_ref[pl.ds(c, 1), :])
-        weight = share_ref[pl.ds(c, 1), :]
-        whole = weight[:, :LANES] + weight[:, LANES:]
-        here = pl.ds(pl.multiple_of(c * LANES, LANES), LANES)
-        for f in range(3):
-            product = values[f] * weight
-            regrid = (product[:, :LANES] + product[:, LANES:]) / whole
-            top = new_ref[f, levels - 1 : levels, here]
-            new_ref[f, levels - 1 : levels, here] = top + rate_ref[0, f] * (regrid - top)
-        return 0
-
-    lax.fori_loop(0, depth // 2, step, 0)
+            couple(f, slice(0, part), helped_ref[f])
+            couple(f, slice(part, 2 * part), own_ref[f])
 
 
 def body(
@@ -331,19 +368,6 @@
         compiler_params=pltpu.CompilerParams(**PARAMS),
         name="pick_sent",
     )(surface, send_rows.reshape(-1, LANES))
-    incoming = pl.pallas_call(
-        functools.partial(exchange_kernel, n),
-        out_shape=jax.ShapeDtypeStruct(outgoing.shape, f32),
-        in_specs=[VMEM],
-        out_specs=VMEM,
-        scratch_shapes=[
-            pltpu.SemaphoreType.DMA((n,)),
-            pltpu.SemaphoreType.DMA((n,)),
-        ],
-        compiler_params=pltpu.CompilerParams(collective_id=0, has_side_effects=True, **PARAMS),
-        name="exchange",
-    )(outgoing)
-
     stepped = pl.pallas_call(
         functools.partial(advance_kernel, x_points, y_points),
         out_shape=jax.ShapeDtypeStruct(state.shape, f32),
@@ -362,12 +386,16 @@
         name="pick_edges",
     )(ocean, ocean_edges.reshape(-1))
 
-    up = [(i, (i + 1) % n) for i in range(n)]
-    down = [(j, i) for i, j in up]
-    eastward = jnp.stack([stepped[:, :, rows - y_points :], rim[:, :, y_points:]])
-    westward = jnp.stack([stepped[:, :, :y_points], rim[:, :, :y_points]])
-    west = lax.ppermute(eastward, "dom", up)
-    east = lax.ppermute(westward, "dom", down)
+    border = jax.ShapeDtypeStruct((3, levels, y_points), f32)
+    incoming, west_a, east_a, west_o, east_o = pl.pallas_call(
+        functools.partial(exchange_kernel, n),
+        out_shape=[jax.ShapeDtypeStruct(outgoing.shape, f32)] + [border] * 4,
+        in_specs=[pl.BlockSpec(memory_space=pl.ANY)] * 3,
+        out_specs=[pl.BlockSpec(memory_space=pl.ANY)] * 5,
+        scratch_shapes=[pltpu.SemaphoreType.DMA((n,))] * 2 + [pltpu.SemaphoreType.DMA((4,))] * 2,
+        compiler_params=pltpu.CompilerParams(collective_id=0, has_side_effects=True, **PARAMS),
+        name="exchange",
+    )(outgoing, stepped, rim)
 
     adjacent = lax.dynamic_slice_in_dim(ocean_adjacent, sec * part, part, 1).reshape(-1)
     kappa = lax.dynamic_slice_in_dim(ocean_kappa, sec * part, part, 0).reshape(1, -1)
@@ -382,13 +410,13 @@
         ],
         compiler_params=pltpu.CompilerParams(**PARAMS),
         name="sweep",
-    )(ocean, west[1], east[1], adjacent, kappa)
+    )(ocean, west_o, east_o, adjacent, kappa)
     helped = lax.ppermute(swept, "sec", [(0, 1)])
 
-    return pl.pallas_call(
-        functools.partial(final_kernel, x_points, y_points),
-        out_shape=jax.ShapeDtypeStruct(state.shape, f32),
-        in_specs=[VMEM] * 3 + [SMEM] + [VMEM] * 5,
+    regrid = pl.pallas_call(
+        regrid_kernel,
+        out_shape=jax.ShapeDtypeStruct((3, rows), f32),
+        in_specs=[VMEM] * 3,
         out_specs=VMEM,
         scratch_shapes=[
             pltpu.VMEM((3 * slots // LANES, 2 * LANES), jnp.bfloat16),
@@ -396,18 +424,18 @@
             pltpu.VMEM((slots // LANES // 2, 2 * LANES), f32),
         ],
         compiler_params=pltpu.CompilerParams(**PARAMS),
+        cost_estimate=pl.CostEstimate(flops=6 * LANES * slots * slots // LANES, bytes_accessed=slots * 20, transcendentals=0),
+        name="regrid",
+    )(incoming, intersection_source.reshape(-1, LANES), intersection_weight.reshape(-1, LANES))
+
+    return pl.pallas_call(
+        functools.partial(finish_kernel, x_points, y_points),
+        out_shape=jax.ShapeDtypeStruct(state.shape, f32),
+        in_specs=[VMEM, SMEM] + [VMEM] * 5,
+        out_specs=VMEM,
+        compiler_params=pltpu.CompilerParams(**PARAMS),
         name="finish",
-    )(
-        incoming,
-        intersection_source.reshape(-1, LANES),
-        intersection_weight.reshape(-1, LANES),
-        couple_rate,
-        stepped,
-        west[0],
-        east[0],
-        swept,
-        helped,
-    )
+    )(regrid, couple_rate, stepped, west_a, east_a, swept, helped)
 
 
 def solution(mesh):

time: 104 us -> 71.5 us (0.69)
  Pallas kernels: 81.7 us -> 62.3 us
  waiting for transfers between devices: 8.2 us -> 0.01 us
  starting transfers between devices: 9.91 us -> 3.46 us
  local copies, waits for them, and re-layouts: 4.07 us -> 5.2 us
    ppermute x2 -> x0, waiting for transfers between devices: 8.19 us -> none  [the longest x1 6.05 us: body(): west = lax.ppermute(eastward, 'dom', up)]
    pallas_call x1, Pallas kernels: 12.5 us -> 4.95 us  [body(): pl.pallas_call(send_kernel, out_shape=jax.ShapeDtypeStruct((n, 3, cap //...]
    ppermute x2 -> x0, starting transfers between devices: 7.04 us -> none  [the longest x1 6.98 us: body(): east = lax.ppermute(westward, 'dom', down)]
    pallas_call x1, Pallas kernels: 32.8 us -> 26.3 us  [body(): pl.pallas_call(sweep_kernel, out_shape=jax.ShapeDtypeStruct((3, levels, p...]
    pallas_call x1, Pallas kernels: 8.24 us -> 3.99 us  [body(): pl.pallas_call(edge_kernel, out_shape=jax.ShapeDtypeStruct((3, levels, 2...]
    pallas_call x2 -> x3, Pallas kernels: 26.1 us -> 24.9 us  [the longest x1 15 us: body(): pl.pallas_call(functools.partial(exchange_kernel, n), out_shape=[jax.Shap...]
    slice x1, local copies, waits for them, and re-layouts: 0.09 us -> 1.22 us  [body(): surface = state[:, levels - 1].reshape(3, rows // LANES, LANES)]
    unnamed x21 -> x23, local copies, waits for them, and re-layouts: 3.81 us -> 3.83 us
  transfers between devices with their start and end apart: 4 -> 2, of which waited for: 2 -> 0; matrix products, arithmetic and copies ran while one was open for 0% -> 2% of each run, Pallas kernels for 21% -> 21%
where the time goes in v2:
time: 71.5 us; the launch traced here: 71.2 us
  Pallas kernels  62.3 us (87%)
  local copies, waits for them, and re-layouts  5.2 us (7%)
  starting transfers between devices  3.46 us (5%)
    pallas_call x1, Pallas kernels, body(): pl.pallas_call(sweep_kernel, out_shape=jax.ShapeDtypeStruct((3, levels, p...  26.3 us
    pallas_call x1, Pallas kernels, body(): pl.pallas_call(functools.partial(exchange_kernel, n), out_shape=[jax.Shap...  15 us
    pallas_call x1, Pallas kernels, body(): pl.pallas_call(regrid_kernel, out_shape=jax.ShapeDtypeStruct((3, rows), f...  7.96 us
    pallas_call x1, Pallas kernels, body(): pl.pallas_call(send_kernel, out_shape=jax.ShapeDtypeStruct((n, 3, cap //...  4.95 us
    pallas_call x1, Pallas kernels, body(): pl.pallas_call(edge_kernel, out_shape=jax.ShapeDtypeStruct((3, levels, 2...  3.99 us
    unnamed x23, local copies, waits for them, and re-layouts  3.83 us
    ppermute x1, starting transfers between devices, body(): helped = lax.ppermute(swept, 'sec', [(0, 1)])  2.04 us
    pallas_call x1, Pallas kernels, body(): pl.pallas_call(functools.partial(advance_kernel, x_points, y_points), out...  2.03 us
  transfers between devices with their start and end apart: 2, of which 0 were waited for; matrix products, arithmetic and copies ran while one was open for 2% of the time, Pallas kernels for 21%

profile of v2, /device:TPU:0, one launch (start us, length us, event | category | flops | bytes accessed | tf_op | source)
XLA Modules:
  0.0 71.2 jit_solution(2463795006674325802)
XLA Ops:
  0.0 0.0 copy-start
  0.0 1.4 %collective-permute-start = (f32[3,8,8192]{2,1,0:T(8,128)}, f32[3,8,8192]{2,1,0:T(8,128)S(1)}, u32[]{:S(2)}, u32[]{:S(2)}) collective-permute-start(f32[3,8,8192]{2,1,0:T(8,128)} %state_ref.1), channel_id=1, source_target_pairs={{16,0},{17,1},{18,2},{19,3},{20,4},{21,5},{22,6},{23,7},{24,8},{25... | collective-permute-start | bytes 2359304 | tf_op jit(solution)/shard_map/ppermute | solution.py:358
  1.4 1.2 %slice.3 = f32[3,1,8192]{2,1,0:T(1,128)S(1)} slice(f32[3,8,8192]{2,1,0:T(8,128)} %state_ref.1), slice={[0:3], [7:8], [0:8192]} | slice | bytes 196608 | tf_op jit(solution)/shard_map/slice | solution.py:361
  2.7 0.0 copy-done
  2.7 0.0 copy-start.8
  2.7 0.0 copy-start.3
  2.7 0.1 reshape.23.adjacent_ref
  2.8 0.7 copy-done.8
  3.5 0.0 copy-start.9
  3.5 0.7 copy-done.9
  4.1 0.0 copy-start.10
  4.1 0.7 copy-done.10
  4.8 0.1 broadcast_in_dim.2.speed_ref
  4.9 0.0 copy-done.3
  4.9 0.0 copy-start.1
  4.9 1.1 %copy-done.1 = f32[3,8,8192]{2,1,0:T(8,128)S(1)} copy-done((f32[3,8,8192]{2,1,0:T(8,128)S(1)}, f32[3,8,8192]{2,1,0:T(8,128)}, u32[]{:S(2)}) %copy-start.1) | copy-done | bytes 786456
  6.0 0.0 copy-start.4
  6.0 0.0 copy-start.2
  6.0 2.0 %advance.1.stepped_ref = f32[3,8,8192]{2,1,0:T(8,128)S(1)} custom-call(f32[3,8,8192]{2,1,0:T(8,128)S(1)} %copy-done.1, f32[2,8192]{1,0:T(2,128)S(1)} %copy-done.3, f32[8,128]{1,0:T(8,128)S(1)} %broadcast_in_dim.2.speed_ref), custom_call_target="tpu_custom_call" | custom-call | tf_op jit(solution)/shard_map/advance/pallas_call | solution.py:371
  8.1 0.0 copy-done.4
  8.1 5.0 %pick_sent.1.out_ref = f32[16,3,8,128]{3,2,1,0:T(8,128)S(1)} custom-call(f32[3,64,128]{2,1,0:T(8,128)S(1)} %bitcast.7, s32[128,128]{1,0:T(8,128)S(1)} %bitcast.9), custom_call_target="tpu_custom_call" | custom-call | tf_op jit(solution)/shard_map/pick_sent/pallas_call | solution.py:362
  13.0 0.0 collective-permute-done
  13.0 0.0 copy-done.2
  13.0 0.1 broadcast_select_fusion.state_ref
  13.1 4.0 %pick_edges.1.rim_ref = f32[3,8,1024]{2,1,0:T(8,128)S(1)} custom-call(f32[3,8,8192]{2,1,0:T(8,128)S(1)} %broadcast_select_fusion.state_ref, s32[1024]{0:T(1024)S(1)} %bitcast.10), custom_call_target="tpu_custom_call" | custom-call | tf_op jit(solution)/shard_map/pick_edges/pallas_call | solution.py:379
  17.1 15.0 %exchange.1 = (f32[16,3,8,128]{3,2,1,0:T(8,128)S(1)}, f32[3,8,512]{2,1,0:T(8,128)S(1)}, f32[3,8,512]{2,1,0:T(8,128)S(1)}, f32[3,8,512]{2,1,0:T(8,128)S(1)}, f32[3,8,512]{2,1,0:T(8,128)S(1)}) custom-call(f32[16,3,8,128]{3,2,1,0:T(8,128)S(1)} %pick_sent.1.out_ref, f32[3,8,8192]{2,1,0:T(8,128)S(1)} %advance.1.stepped_ref, f32[3,8,1024]{2,1,0:T(8,128)S(1)} %pick_edges.1.rim_ref), custom_call_target="tpu_custom_call" | custom-call | tf_op jit(solution)/shard_map/exchange/pallas_call | solution.py:390
  32.2 0.0 copy-start.6
  32.2 0.0 copy-start.7
  32.2 26.3 %sweep.1.own_ref = f32[3,8,4096]{2,1,0:T(8,128)S(1)} custom-call(f32[3,8,8192]{2,1,0:T(8,128)S(1)} %broadcast_select_fusion.state_ref, f32[3,8,512]{2,1,0:T(8,128)S(1)} %get-tuple-element.13.west_ref, f32[3,8,512]{2,1,0:T(8,128)S(1)} %get-tuple-element.14.east_ref, s32[24576]{0:T(1024)S(1)} %reshape.23.adjacent_ref, f32[1,4096]{1,0:T(1,128)S(1)} %bitcast.8), custom_call_target="tpu_custom_call" | custom-call | tf_op jit(solution)/shard_map/sweep/pallas_call | solution.py:402
  58.6 2.0 %collective-permute-start.1 = (f32[3,8,4096]{2,1,0:T(8,128)S(1)}, f32[3,8,4096]{2,1,0:T(8,128)S(1)}, u32[]{:S(2)}, u32[]{:S(2)}) collective-permute-start(f32[3,8,4096]{2,1,0:T(8,128)S(1)} %sweep.1.own_ref), channel_id=1, source_target_pairs={{0,16},{1,17},{2,18},{3,19},{4,20},{5,21},{6,22},{7,23},{8,24},{9,... | collective-permute-start | bytes 1179656 | tf_op jit(solution)/shard_map/ppermute | solution.py:414
  60.6 0.0 copy-done.6
  60.6 0.0 copy-done.7
  60.6 8.0 %regrid.1.regrid_ref = f32[3,8192]{1,0:T(4,128)S(1)} custom-call(f32[16,3,8,128]{3,2,1,0:T(8,128)S(1)} %get-tuple-element.10.incoming_ref, s32[128,128]{1,0:T(8,128)S(1)} %bitcast.11, f32[128,128]{1,0:T(8,128)S(1)} %bitcast.12), custom_call_target="tpu_custom_call" | custom-call | flops 1610612736 | bytes 327680 | tf_op jit(solution)/shard_map/regrid/pallas_call | solution.py:416
  68.6 0.0 collective-permute-done.1.helped_ref
  68.6 0.0 copy-start.5
  68.6 0.6 copy-done.5
  69.3 1.9 %finish.1 = f32[3,8,8192]{2,1,0:T(8,128)} custom-call(f32[3,8192]{1,0:T(4,128)S(1)} %regrid.1.regrid_ref, f32[1,3]{1,0:T(1,128)S(1)} %copy-done.5, f32[3,8,8192]{2,1,0:T(8,128)S(1)} %advance.1.stepped_ref, f32[3,8,512]{2,1,0:T(8,128)S(1)} %get-tuple-element.11.west_ref, f32[3,8,512]{2,1,0:T(8,128)S(1)} %get-tuple-element.12.east_ref, ...), custom_call_target="tpu_custom_call" | custom-call | tf_op jit(solution)/shard_map/finish/pallas_call | solution.py:431
  (3 shorter events, 0.0 us)
Async XLA Ops:
  0.0 2.7 %copy-start = (s32[6,8192]{1,0:T(8,128)S(1)}, s32[6,8192]{1,0:T(8,128)}, u32[]{:S(2)}) copy-start(s32[6,8192]{1,0:T(8,128)} %param.17) | copy-start | bytes 589828
  0.0 13.0 %collective-permute-start = (f32[3,8,8192]{2,1,0:T(8,128)}, f32[3,8,8192]{2,1,0:T(8,128)S(1)}, u32[]{:S(2)}, u32[]{:S(2)}) collective-permute-start(f32[3,8,8192]{2,1,0:T(8,128)} %state_ref.1), channel_id=1, source_target_pairs={{16,0},{17,1},{18,2},{19,3},{20,4},{21,5},{22,6},{23,7},{24,8},{25... | collective-permute-start | bytes 2359304 | tf_op jit(solution)/shard_map/ppermute | solution.py:358
  2.7 0.8 %copy-start.8 = (f32[8192]{0:T(1024)S(1)}, f32[8192]{0:T(1024)}, u32[]{:S(2)}) copy-start(f32[8192]{0:T(1024)} %param.19) | copy-start | bytes 98308
  2.7 2.2 %copy-start.3 = (f32[2,8192]{1,0:T(2,128)S(1)}, f32[2,8192]{1,0:T(2,128)}, u32[]{:S(2)}) copy-start(f32[2,8192]{1,0:T(2,128)} %metric_ref.1) | copy-start | bytes 196612
  3.5 0.7 copy-start.9
  4.1 0.7 copy-start.10
  4.9 1.1 %copy-start.1 = (f32[3,8,8192]{2,1,0:T(8,128)S(1)}, f32[3,8,8192]{2,1,0:T(8,128)}, u32[]{:S(2)}) copy-start(f32[3,8,8192]{2,1,0:T(8,128)} %state_ref.1) | copy-start | bytes 2359300
  6.0 2.0 %copy-start.4 = (s32[16384]{0:T(1024)S(1)}, s32[16384]{0:T(1024)}, u32[]{:S(2)}) copy-start(s32[16384]{0:T(1024)} %param.11) | copy-start | bytes 196612
  6.0 7.0 %copy-start.2 = (f32[3,8,8192]{2,1,0:T(8,128)S(1)}, f32[3,8,8192]{2,1,0:T(8,128)}, u32[]{:S(2)}) copy-start(f32[3,8,8192]{2,1,0:T(8,128)} %state_ref.1) | copy-start | bytes 2359300
  32.2 28.4 %copy-start.6 = (s32[16384]{0:T(1024)S(1)}, s32[16384]{0:T(1024)}, u32[]{:S(2)}) copy-start(s32[16384]{0:T(1024)} %param.12) | copy-start | bytes 196612
  32.2 28.4 %copy-start.7 = (f32[16384]{0:T(1024)S(1)}, f32[16384]{0:T(1024)}, u32[]{:S(2)}) copy-start(f32[16384]{0:T(1024)} %param.13) | copy-start | bytes 196612
  58.6 10.0 %collective-permute-start.1 = (f32[3,8,4096]{2,1,0:T(8,128)S(1)}, f32[3,8,4096]{2,1,0:T(8,128)S(1)}, u32[]{:S(2)}, u32[]{:S(2)}) collective-permute-start(f32[3,8,4096]{2,1,0:T(8,128)S(1)} %sweep.1.own_ref), channel_id=1, source_target_pairs={{0,16},{1,17},{2,18},{3,19},{4,20},{5,21},{6,22},{7,23},{8,24},{9,... | collective-permute-start | bytes 1179656 | tf_op jit(solution)/shard_map/ppermute | solution.py:414
  68.6 0.7 copy-start.5

commit v3 on v2

--- a/solution.py
+++ b/solution.py
@@ -49,93 +49,6 @@
     ]
 
 
-def send_kernel(surface_ref, rows_ref, out_ref, terms_ref):
-    depth = surface_ref.shape[1]
-    for f in range(3):
-        terms_ref[f * depth : (f + 1) * depth, :] = two_terms(surface_ref[f])
-    per_peer = out_ref.shape[2]
-
-    def step(i, _):
-        index = jnp.concatenate([rows_ref[pl.ds(2 * i, 1), :], rows_ref[pl.ds(2 * i + 1, 1), :]], axis=1)
-        values = pick(terms_ref[...], depth, index)
-        for k in range(2):
-            place = 2 * i + k
-            for f in range(3):
-                out_ref[place // per_peer, f, pl.ds(place % per_peer, 1), :] = values[f][
-                    :, k * LANES : (k + 1) * LANES
-                ]
-        return 0
-
-    lax.fori_loop(0, rows_ref.shape[0] // 2, step, 0, unroll=4)
-
-
-def exchange_kernel(
-    n, out_ref, stepped_ref, rim_ref, in_ref, west_a_ref, east_a_ref, west_o_ref, east_o_ref,
-    send_sem, recv_sem, edge_send_sem, edge_recv_sem,
-):
-    sec, dom = lax.axis_index("sec"), lax.axis_index("dom")
-    right, left = lax.rem(dom + 1, n), lax.rem(dom + n - 1, n)
-    mesh_ids = pl.DeviceIdType.MESH
-    barrier = pltpu.get_barrier_semaphore()
-
-    def greet(p, _):
-        pl.semaphore_signal(barrier, inc=1, device_id=(1 - sec, p), device_id_type=mesh_ids)
-        return 0
-
-    lax.fori_loop(0, n, greet, 0)
-    for side in (left, right):
-        pl.semaphore_signal(barrier, inc=1, device_id=(sec, side), device_id_type=mesh_ids)
-    pl.semaphore_wait(barrier, n + 2)
-
-    edge, rows = west_a_ref.shape[2], stepped_ref.shape[2]
-    first, last = pl.ds(0, edge), pl.ds(rows - edge, edge)
-    edges = []
-    for k, (source, target, side) in enumerate(
-        (
-            (rim_ref.at[:, :, pl.ds(edge, edge)], west_o_ref, right),
-            (rim_ref.at[:, :, first], east_o_ref, left),
-            (stepped_ref.at[:, :, last], west_a_ref, right),
-            (stepped_ref.at[:, :, first], east_a_ref, left),
-        )
-    ):
-        edges.append(
-            pltpu.make_async_remote_copy(
-                src_ref=source,
-                dst_ref=target,
-                send_sem=edge_send_sem.at[k],
-                recv_sem=edge_recv_sem.at[k],
-                device_id=(sec, side),
-                device_id_type=mesh_ids,
-            )
-        )
-
-    def copy(k):
-        p = lax.rem(dom + k, n)
-        return pltpu.make_async_remote_copy(
-            src_ref=out_ref.at[p],
-            dst_ref=in_ref.at[dom],
-            send_sem=send_sem.at[k],
-            recv_sem=recv_sem.at[k],
-            device_id=(1 - sec, p),
-            device_id_type=mesh_ids,
-        )
-
-    def start(k, _):
-        copy(k).start()
-        return 0
-
-    def wait(k, _):
-        copy(k).wait()
-        return 0
-
-    for each in edges:
-        each.start()
-    lax.fori_loop(0, n, start, 0)
-    lax.fori_loop(0, n, wait, 0)
-    for each in edges:
-        each.wait()
-
-
 def lane_phase(shape):
     return lax.broadcasted_iota(jnp.int32, shape, 1) % 4
 
@@ -153,37 +66,30 @@
     return total
 
 
-def advance_kernel(x_points, y_points, state_ref, metric_ref, speed_ref, stepped_ref):
-    @pl.when(lax.axis_index("sec") == 0)
-    def _():
-        def piece(g, _):
-            def at(i, f):
-                return state_ref[f, :, pl.ds(pl.multiple_of(start + i * y_points, LANES), LANES)]
-
-            start = (g // (y_points // LANES)) * 4 * y_points + (g % (y_points // LANES)) * LANES
-            phase = lane_phase((state_ref.shape[1], LANES))
-            u = [at(i, 0) for i in range(4)]
-            v = [at(i, 1) for i in range(4)]
-            h = [at(i, 2) for i in range(4)]
-            speed = speed_ref[...]
-            for i in range(4):
-                here = pl.ds(pl.multiple_of(start + i * y_points, LANES), LANES)
-                gx = metric_ref[0:1, here]
-                gy = metric_ref[1:2, here]
-                dx_h = sum(np.float32(DERIVATIVE[i, j]) * h[j] for j in range(4))
-                dx_u = sum(np.float32(DERIVATIVE[i, j]) * u[j] for j in range(4))
-                stepped_ref[0, :, here] = u[i] - TIME_STEP * (gx * dx_h)
-                stepped_ref[1, :, here] = v[i] - TIME_STEP * (gy * along_second(h[i], phase))
-                spread = gx * dx_u + gy * along_second(v[i], phase)
-                stepped_ref[2, :, here] = h[i] - TIME_STEP * speed * spread
-            return 0
-
-        lax.fori_loop(0, x_points // 4 * (y_points // LANES), piece, 0)
-
-    @pl.when(lax.axis_index("sec") == 1)
-    def _():
-        for f in range(3):
-            stepped_ref[f] = state_ref[f]
+def advance(x_points, y_points, state_ref, metric_ref, speed_ref, stepped_ref):
+    def piece(g, _):
+        def at(i, f):
+            return state_ref[f, :, pl.ds(pl.multiple_of(start + i * y_points, LANES), LANES)]
+
+        start = (g // (y_points // LANES)) * 4 * y_points + (g % (y_points // LANES)) * LANES
+        phase = lane_phase((state_ref.shape[1], LANES))
+        u = [at(i, 0) for i in range(4)]
+        v = [at(i, 1) for i in range(4)]
+        h = [at(i, 2) for i in range(4)]
+        speed = speed_ref[...]
+        for i in range(4):
+            here = pl.ds(pl.multiple_of(start + i * y_points, LANES), LANES)
+            gx = metric_ref[0:1, here]
+            gy = metric_ref[1:2, here]
+            dx_h = sum(np.float32(DERIVATIVE[i, j]) * h[j] for j in range(4))
+            dx_u = sum(np.float32(DERIVATIVE[i, j]) * u[j] for j in range(4))
+            stepped_ref[0, :, here] = u[i] - TIME_STEP * (gx * dx_h)
+            stepped_ref[1, :, here] = v[i] - TIME_STEP * (gy * along_second(h[i], phase))
+            spread = gx * dx_u + gy * along_second(v[i], phase)
+            stepped_ref[2, :, here] = h[i] - TIME_STEP * speed * spread
+        return 0
+
+    lax.fori_loop(0, x_points // 4 * (y_points // LANES), piece, 0)
 
 
 def to_rows(source_ref, source_at, table_ref, table_at, count):
@@ -202,10 +108,9 @@
     return [block[f * levels : (f + 1) * levels] for f in range(3)]
 
 
-def edge_kernel(state_ref, edges_ref, border_ref, table_ref, picked_ref):
-    rows = state_ref.shape[2]
+def pick_edges(state_ref, edges_ref, border_ref, table_ref, picked_ref):
     count = edges_ref.shape[0]
-    to_rows(state_ref, 0, table_ref, 0, rows)
+    to_rows(state_ref, 0, table_ref, 0, state_ref.shape[2])
 
     def step(i, _):
         base = i * 16
@@ -219,6 +124,123 @@
         block = from_rows(picked_ref, c * LANES, state_ref.shape[1])
         for f in range(3):
             border_ref[f, :, c * LANES : (c + 1) * LANES] = block[f]
+
+
+def prepare_kernel(
+    n, x_points, y_points, surface_ref, rows_ref, state_ref, edges_ref, metric_ref, speed_ref,
+    in_ref, stepped_ref, west_a_ref, east_a_ref, west_o_ref, east_o_ref,
+    terms_ref, out_ref, rim_ref, table_ref, picked_ref, send_sem, recv_sem, edge_send_sem, edge_recv_sem,
+):
+    sec, dom = lax.axis_index("sec"), lax.axis_index("dom")
+    right, left = lax.rem(dom + 1, n), lax.rem(dom + n - 1, n)
+    mesh_ids = pl.DeviceIdType.MESH
+    barrier = pltpu.get_barrier_semaphore()
+
+    def greet(p, _):
+        pl.semaphore_signal(barrier, inc=1, device_id=(1 - sec, p), device_id_type=mesh_ids)
+        return 0
+
+    lax.fori_loop(0, n, greet, 0)
+    for side in (left, right):
+        pl.semaphore_signal(barrier, inc=1, device_id=(sec, side), device_id_type=mesh_ids)
+
+    @pl.when(sec == 0)
+    def _():
+        advance(x_points, y_points, state_ref, metric_ref, speed_ref, stepped_ref)
+
+    @pl.when(sec == 1)
+    def _():
+        pick_edges(state_ref, edges_ref, rim_ref, table_ref, picked_ref)
+
+    pl.semaphore_wait(barrier, n + 2)
+
+    rows = state_ref.shape[2]
+    first, last = pl.ds(0, y_points), pl.ds(rows - y_points, y_points)
+
+    def edge(k, source, target, arrival, device):
+        return pltpu.make_async_remote_copy(
+            src_ref=source,
+            dst_ref=target,
+            send_sem=edge_send_sem.at[k],
+            recv_sem=edge_recv_sem.at[arrival],
+            device_id=device,
+            device_id_type=mesh_ids,
+        )
+
+    rim_last, rim_first = rim_ref.at[:, :, pl.ds(y_points, y_points)], rim_ref.at[:, :, first]
+    ocean_edges = [
+        edge(0, rim_last, west_o_ref, 0, (1, right)),
+        edge(1, rim_first, east_o_ref, 1, (1, left)),
+        edge(2, rim_last, west_o_ref, 0, (0, right)),
+        edge(3, rim_first, east_o_ref, 1, (0, left)),
+    ]
+    atmosphere_edges = [
+        edge(0, stepped_ref.at[:, :, last], west_a_ref, 2, (0, right)),
+        edge(1, stepped_ref.at[:, :, first], east_a_ref, 3, (0, left)),
+    ]
+
+    @pl.when(sec == 0)
+    def _():
+        for each in atmosphere_edges:
+            each.start()
+
+    @pl.when(sec == 1)
+    def _():
+        for each in ocean_edges:
+            each.start()
+
+    depth = surface_ref.shape[1]
+    for f in range(3):
+        terms_ref[f * depth : (f + 1) * depth, :] = two_terms(surface_ref[f])
+    per_peer = out_ref.shape[2]
+
+    def copy(k):
+        p = lax.rem(dom + k, n)
+        return pltpu.make_async_remote_copy(
+            src_ref=out_ref.at[p],
+            dst_ref=in_ref.at[dom],
+            send_sem=send_sem.at[k],
+            recv_sem=recv_sem.at[k],
+            device_id=(1 - sec, p),
+            device_id_type=mesh_ids,
+        )
+
+    def start(k, _):
+        p = lax.rem(dom + k, n)
+        for i in range(per_peer // 2):
+            place = p * per_peer + 2 * i
+            index = jnp.concatenate(
+                [rows_ref[pl.ds(place, 1), :], rows_ref[pl.ds(place + 1, 1), :]], axis=1
+            )
+            values = pick(terms_ref[...], depth, index)
+            for f in range(3):
+                for half in range(2):
+                    out_ref[p, f, 2 * i + half : 2 * i + half + 1, :] = values[f][
+                        :, half * LANES : (half + 1) * LANES
+                    ]
+        copy(k).start()
+        return 0
+
+    def wait(k, _):
+        copy(k).wait()
+        return 0
+
+    lax.fori_loop(0, n, start, 0)
+    lax.fori_loop(0, n, wait, 0)
+
+    @pl.when(sec == 0)
+    def _():
+        for each in atmosphere_edges:
+            each.wait()
+        ocean_edges[0].wait_recv()
+        ocean_edges[1].wait_recv()
+
+    @pl.when(sec == 1)
+    def _():
+        for each in ocean_edges:
+            each.wait_send()
+        ocean_edges[0].wait_recv()
+        ocean_edges[1].wait_recv()
 
 
 def sweep_kernel(state_ref, west_ref, east_ref, adjacent_ref, kappa_ref, swept_ref, table_ref, sum_ref):
@@ -359,43 +381,37 @@
     ocean = jnp.where(sec == 0, ocean, state)
 
     surface = state[:, levels - 1].reshape(3, rows // LANES, LANES)
-    outgoing = pl.pallas_call(
-        send_kernel,
-        out_shape=jax.ShapeDtypeStruct((n, 3, cap // LANES, LANES), f32),
-        in_specs=[VMEM] * 2,
-        out_specs=VMEM,
-        scratch_shapes=[pltpu.VMEM((3 * rows // LANES, 2 * LANES), jnp.bfloat16)],
-        compiler_params=pltpu.CompilerParams(**PARAMS),
-        name="pick_sent",
-    )(surface, send_rows.reshape(-1, LANES))
-    stepped = pl.pallas_call(
-        functools.partial(advance_kernel, x_points, y_points),
-        out_shape=jax.ShapeDtypeStruct(state.shape, f32),
-        in_specs=[VMEM] * 3,
-        out_specs=VMEM,
-        compiler_params=pltpu.CompilerParams(**PARAMS),
-        name="advance",
-    )(state, atm_metric, jnp.broadcast_to(wave_speed[:, None], (levels, LANES)))
-    rim = pl.pallas_call(
-        edge_kernel,
-        out_shape=jax.ShapeDtypeStruct((3, levels, 2 * y_points), f32),
-        in_specs=[VMEM, SMEM],
-        out_specs=VMEM,
-        scratch_shapes=[pltpu.VMEM((rows, LANES), f32), pltpu.VMEM((2 * y_points, LANES), f32)],
-        compiler_params=pltpu.CompilerParams(**PARAMS),
-        name="pick_edges",
-    )(ocean, ocean_edges.reshape(-1))
-
     border = jax.ShapeDtypeStruct((3, levels, y_points), f32)
-    incoming, west_a, east_a, west_o, east_o = pl.pallas_call(
-        functools.partial(exchange_kernel, n),
-        out_shape=[jax.ShapeDtypeStruct(outgoing.shape, f32)] + [border] * 4,
-        in_specs=[pl.BlockSpec(memory_space=pl.ANY)] * 3,
-        out_specs=[pl.BlockSpec(memory_space=pl.ANY)] * 5,
-        scratch_shapes=[pltpu.SemaphoreType.DMA((n,))] * 2 + [pltpu.SemaphoreType.DMA((4,))] * 2,
+    arriving = jax.ShapeDtypeStruct((n, 3, cap // LANES, LANES), f32)
+    incoming, stepped, west_a, east_a, west_o, east_o = pl.pallas_call(
+        functools.partial(prepare_kernel, n, x_points, y_points),
+        out_shape=[arriving, jax.ShapeDtypeStruct(state.shape, f32)] + [border] * 4,
+        in_specs=[VMEM] * 3 + [SMEM] + [VMEM] * 2,
+        out_specs=[VMEM] * 6,
+        scratch_shapes=[
+            pltpu.VMEM((3 * rows // LANES, 2 * LANES), jnp.bfloat16),
+            pltpu.VMEM(arriving.shape, f32),
+            pltpu.VMEM((3, levels, 2 * y_points), f32),
+            pltpu.VMEM((rows, LANES), f32),
+            pltpu.VMEM((2 * y_points, LANES), f32),
+            pltpu.SemaphoreType.DMA((n,)),
+            pltpu.SemaphoreType.DMA((n,)),
+            pltpu.SemaphoreType.DMA((4,)),
+            pltpu.SemaphoreType.DMA((4,)),
+        ],
         compiler_params=pltpu.CompilerParams(collective_id=0, has_side_effects=True, **PARAMS),
-        name="exchange",
-    )(outgoing, stepped, rim)
+        cost_estimate=pl.CostEstimate(
+            flops=6 * rows * LANES * slots // LANES, bytes_accessed=3 * state.size * 4, transcendentals=0
+        ),
+        name="prepare",
+    )(
+        surface,
+        send_rows.reshape(-1, LANES),
+        state,
+        ocean_edges.reshape(-1),
+        atm_metric,
+        jnp.broadcast_to(wave_speed[:, None], (levels, LANES)),
+    )
 
     adjacent = lax.dynamic_slice_in_dim(ocean_adjacent, sec * part, part, 1).reshape(-1)
     kappa = lax.dynamic_slice_in_dim(ocean_kappa, sec * part, part, 0).reshape(1, -1)

time: 71.5 us -> 61.1 us (0.85)
  Pallas kernels: 62.3 us -> 52.5 us
    pallas_call x4 -> x1, Pallas kernels: 26 us -> 16.3 us  [body(): pl.pallas_call(functools.partial(prepare_kernel, n, x_points, y_points),...]
  transfers between devices with their start and end apart: 2 -> 2, of which waited for: 0 -> 0; matrix products, arithmetic and copies ran while one was open for 2% -> 2% of each run, Pallas kernels for 21% -> 40%
where the time goes in v3:
time: 61.1 us; the launch traced here: 60.8 us
  Pallas kernels  52.5 us (86%)
  local copies, waits for them, and re-layouts  4.58 us (7%)
  starting transfers between devices  3.36 us (5%)
    pallas_call x1, Pallas kernels, body(): pl.pallas_call(sweep_kernel, out_shape=jax.ShapeDtypeStruct((3, levels, p...  26.3 us
    pallas_call x1, Pallas kernels, body(): pl.pallas_call(functools.partial(prepare_kernel, n, x_points, y_points),...  16.3 us
    pallas_call x1, Pallas kernels, body(): pl.pallas_call(regrid_kernel, out_shape=jax.ShapeDtypeStruct((3, rows), f...  7.96 us
    unnamed x23, local copies, waits for them, and re-layouts  3.21 us
    ppermute x1, starting transfers between devices, body(): helped = lax.ppermute(swept, 'sec', [(0, 1)])  1.95 us
    pallas_call x1, Pallas kernels, body(): pl.pallas_call(functools.partial(finish_kernel, x_points, y_points), out_...  1.93 us
    ppermute x1, starting transfers between devices, body(): ocean = lax.ppermute(state, 'sec', [(1, 0)])  1.41 us
    slice x1, local copies, waits for them, and re-layouts, body(): surface = state[:, levels - 1].reshape(3, rows // LANES, LANES)  1.22 us
  transfers between devices with their start and end apart: 2, of which 0 were waited for; matrix products, arithmetic and copies ran while one was open for 2% of the time, Pallas kernels for 40%

profile of v3, /device:TPU:0, one launch (start us, length us, event | category | flops | bytes accessed | tf_op | source)
XLA Modules:
  0.0 60.8 jit_solution(18342715225923002261)
XLA Ops:
  0.0 0.0 copy-start
  0.0 1.4 %collective-permute-start = (f32[3,8,8192]{2,1,0:T(8,128)}, f32[3,8,8192]{2,1,0:T(8,128)S(1)}, u32[]{:S(2)}, u32[]{:S(2)}) collective-permute-start(f32[3,8,8192]{2,1,0:T(8,128)} %state_ref.1), channel_id=1, source_target_pairs={{16,0},{17,1},{18,2},{19,3},{20,4},{21,5},{22,6},{23,7},{24,8},{25... | collective-permute-start | bytes 2359304 | tf_op jit(solution)/shard_map/ppermute | solution.py:380
  1.4 0.0 copy-start.8
  1.4 1.2 %slice.3 = f32[3,1,8192]{2,1,0:T(1,128)S(1)} slice(f32[3,8,8192]{2,1,0:T(8,128)} %state_ref.1), slice={[0:3], [7:8], [0:8192]} | slice | bytes 196608 | tf_op jit(solution)/shard_map/slice | solution.py:383
  2.7 0.0 copy-start.9
  2.7 0.7 %copy-done.9 = s32[2,512]{1,0:T(2,128)S(1)} copy-done((s32[2,512]{1,0:T(2,128)S(1)}, s32[2,512]{1,0:T(2,128)}, u32[]{:S(2)}) %copy-start.9) | copy-done | bytes 4120
  3.4 0.0 copy-done.8
  3.4 0.0 copy-done
  3.4 0.0 copy-start.4
  3.4 0.0 copy-start.5
  3.4 0.1 reshape.23.adjacent_ref
  3.5 0.0 copy-start.10
  3.5 0.6 %copy-done.10 = f32[8]{0:T(128)S(1)} copy-done((f32[8]{0:T(128)S(1)}, f32[8]{0:T(128)}, u32[]{:S(2)}) %copy-start.10) | copy-done | bytes 56
  4.1 0.1 broadcast_in_dim.2.speed_ref
  4.2 0.0 copy-done.4
  4.2 0.0 copy-done.5
  4.3 0.0 copy-start.1
  4.3 1.1 %copy-done.1 = f32[3,8,8192]{2,1,0:T(8,128)S(1)} copy-done((f32[3,8,8192]{2,1,0:T(8,128)S(1)}, f32[3,8,8192]{2,1,0:T(8,128)}, u32[]{:S(2)}) %copy-start.1) | copy-done | bytes 786456
  5.4 0.0 copy-start.2
  5.4 16.3 %prepare.1 = (f32[16,3,8,128]{3,2,1,0:T(8,128)S(1)}, f32[3,8,8192]{2,1,0:T(8,128)S(1)}, f32[3,8,512]{2,1,0:T(8,128)S(1)}, f32[3,8,512]{2,1,0:T(8,128)S(1)}, f32[...) custom-call(f32[3,64,128]{2,1,0:T(8,128)S(1)} %bitcast.7, s32[128,128]{1,0:T(8,128)S(1)} %bitcast.10, ...), custom_call_target="tpu_custom_call" | custom-call | flops 805306368 | bytes 2359296 | tf_op jit(solution)/shard_map/prepare/pallas_call | solution.py:386
  21.7 0.0 collective-permute-done
  21.7 0.0 copy-done.2
  21.7 0.1 broadcast_select_fusion.state_ref
  21.8 0.0 copy-start.6
  21.8 0.0 copy-start.7
  21.9 26.3 %sweep.1.own_ref = f32[3,8,4096]{2,1,0:T(8,128)S(1)} custom-call(f32[3,8,8192]{2,1,0:T(8,128)S(1)} %broadcast_select_fusion.state_ref, f32[3,8,512]{2,1,0:T(8,128)S(1)} %get-tuple-element.15.west_ref, f32[3,8,512]{2,1,0:T(8,128)S(1)} %get-tuple-element.16.east_ref, s32[24576]{0:T(1024)S(1)} %reshape.23.adjacent_ref, f32[1,4096]{1,0:T(1,128)S(1)} %bitcast.8), custom_call_target="tpu_custom_call" | custom-call | tf_op jit(solution)/shard_map/sweep/pallas_call | solution.py:418
  48.2 1.9 %collective-permute-start.1 = (f32[3,8,4096]{2,1,0:T(8,128)S(1)}, f32[3,8,4096]{2,1,0:T(8,128)S(1)}, u32[]{:S(2)}, u32[]{:S(2)}) collective-permute-start(f32[3,8,4096]{2,1,0:T(8,128)S(1)} %sweep.1.own_ref), channel_id=1, source_target_pairs={{0,16},{1,17},{2,18},{3,19},{4,20},{5,21},{6,22},{7,23},{8,24},{9,... | collective-permute-start | bytes 1179656 | tf_op jit(solution)/shard_map/ppermute | solution.py:430
  50.2 0.0 copy-done.6
  50.2 0.0 copy-done.7
  50.2 8.0 %regrid.1.regrid_ref = f32[3,8192]{1,0:T(4,128)S(1)} custom-call(f32[16,3,8,128]{3,2,1,0:T(8,128)S(1)} %get-tuple-element.11.incoming_ref, s32[128,128]{1,0:T(8,128)S(1)} %bitcast.11, f32[128,128]{1,0:T(8,128)S(1)} %bitcast.12), custom_call_target="tpu_custom_call" | custom-call | flops 1610612736 | bytes 327680 | tf_op jit(solution)/shard_map/regrid/pallas_call | solution.py:432
  58.2 0.0 collective-permute-done.1.helped_ref
  58.2 0.0 copy-start.3
  58.2 0.6 %copy-done.3 = f32[1,3]{1,0:T(1,128)S(1)} copy-done((f32[1,3]{1,0:T(1,128)S(1)}, f32[1,3]{1,0:T(1,128)}, u32[]{:S(2)}) %copy-start.3) | copy-done | bytes 36
  58.8 1.9 %finish.1 = f32[3,8,8192]{2,1,0:T(8,128)} custom-call(f32[3,8192]{1,0:T(4,128)S(1)} %regrid.1.regrid_ref, f32[1,3]{1,0:T(1,128)S(1)} %copy-done.3, f32[3,8,8192]{2,1,0:T(8,128)S(1)} %get-tuple-element.12.stepped_ref, f32[3,8,512]{2,1,0:T(8,128)S(1)} %get-tuple-element.13.west_ref, f32[3,8,512]{2,1,0:T(8,128)S(1)} %get-tuple-element.14.east_ref, ...), custom_call_target="tpu_custom_call" | custom-call | tf_op jit(solution)/shard_map/finish/pallas_call | solution.py:447
  (3 shorter events, 0.0 us)
Async XLA Ops:
  0.0 3.4 %copy-start = (s32[6,8192]{1,0:T(8,128)S(1)}, s32[6,8192]{1,0:T(8,128)}, u32[]{:S(2)}) copy-start(s32[6,8192]{1,0:T(8,128)} %param.17) | copy-start | bytes 589828
  0.0 21.7 %collective-permute-start = (f32[3,8,8192]{2,1,0:T(8,128)}, f32[3,8,8192]{2,1,0:T(8,128)S(1)}, u32[]{:S(2)}, u32[]{:S(2)}) collective-permute-start(f32[3,8,8192]{2,1,0:T(8,128)} %state_ref.1), channel_id=1, source_target_pairs={{16,0},{17,1},{18,2},{19,3},{20,4},{21,5},{22,6},{23,7},{24,8},{25... | collective-permute-start | bytes 2359304 | tf_op jit(solution)/shard_map/ppermute | solution.py:380
  1.4 1.9 %copy-start.8 = (f32[8192]{0:T(1024)S(1)}, f32[8192]{0:T(1024)}, u32[]{:S(2)}) copy-start(f32[8192]{0:T(1024)} %param.19) | copy-start | bytes 98308
  2.7 0.7 %copy-start.9 = (s32[2,512]{1,0:T(2,128)S(1)}, s32[2,512]{1,0:T(2,128)}, u32[]{:S(2)}) copy-start(s32[2,512]{1,0:T(2,128)} %param.18) | copy-start | bytes 12292
  3.4 0.8 %copy-start.4 = (s32[16384]{0:T(1024)S(1)}, s32[16384]{0:T(1024)}, u32[]{:S(2)}) copy-start(s32[16384]{0:T(1024)} %param.11) | copy-start | bytes 196612
  3.4 0.9 %copy-start.5 = (f32[2,8192]{1,0:T(2,128)S(1)}, f32[2,8192]{1,0:T(2,128)}, u32[]{:S(2)}) copy-start(f32[2,8192]{1,0:T(2,128)} %metric_ref.1) | copy-start | bytes 196612
  3.5 0.7 %copy-start.10 = (f32[8]{0:T(128)S(1)}, f32[8]{0:T(128)}, u32[]{:S(2)}) copy-start(f32[8]{0:T(128)} %param.16) | copy-start | bytes 100
  4.3 1.1 %copy-start.1 = (f32[3,8,8192]{2,1,0:T(8,128)S(1)}, f32[3,8,8192]{2,1,0:T(8,128)}, u32[]{:S(2)}) copy-start(f32[3,8,8192]{2,1,0:T(8,128)} %state_ref.1) | copy-start | bytes 2359300
  5.4 16.3 %copy-start.2 = (f32[3,8,8192]{2,1,0:T(8,128)S(1)}, f32[3,8,8192]{2,1,0:T(8,128)}, u32[]{:S(2)}) copy-start(f32[3,8,8192]{2,1,0:T(8,128)} %state_ref.1) | copy-start | bytes 2359300
  21.8 28.3 %copy-start.6 = (s32[16384]{0:T(1024)S(1)}, s32[16384]{0:T(1024)}, u32[]{:S(2)}) copy-start(s32[16384]{0:T(1024)} %param.12) | copy-start | bytes 196612
  21.8 28.3 %copy-start.7 = (f32[16384]{0:T(1024)S(1)}, f32[16384]{0:T(1024)}, u32[]{:S(2)}) copy-start(f32[16384]{0:T(1024)} %param.13) | copy-start | bytes 196612
  48.2 9.9 %collective-permute-start.1 = (f32[3,8,4096]{2,1,0:T(8,128)S(1)}, f32[3,8,4096]{2,1,0:T(8,128)S(1)}, u32[]{:S(2)}, u32[]{:S(2)}) collective-permute-start(f32[3,8,4096]{2,1,0:T(8,128)S(1)} %sweep.1.own_ref), channel_id=1, source_target_pairs={{0,16},{1,17},{2,18},{3,19},{4,20},{5,21},{6,22},{7,23},{8,24},{9,... | collective-permute-start | bytes 1179656 | tf_op jit(solution)/shard_map/ppermute | solution.py:430
  58.2 0.7 %copy-start.3 = (f32[1,3]{1,0:T(1,128)S(1)}, f32[1,3]{1,0:T(1,128)}, u32[]{:S(2)}) copy-start(f32[1,3]{1,0:T(1,128)} %rate_ref.1) | copy-start | bytes 40

commit v4 on v3

--- a/solution.py
+++ b/solution.py
@@ -67,6 +67,11 @@
 
 
 def advance(x_points, y_points, state_ref, metric_ref, speed_ref, stepped_ref):
+    level = lax.broadcasted_iota(jnp.int32, (state_ref.shape[1], LANES), 0)
+    speed = jnp.zeros(level.shape, jnp.float32)
+    for k in range(level.shape[0]):
+        speed = jnp.where(level == k, speed_ref[k], speed)
+
     def piece(g, _):
         def at(i, f):
             return state_ref[f, :, pl.ds(pl.multiple_of(start + i * y_points, LANES), LANES)]
@@ -76,7 +81,6 @@
         u = [at(i, 0) for i in range(4)]
         v = [at(i, 1) for i in range(4)]
         h = [at(i, 2) for i in range(4)]
-        speed = speed_ref[...]
         for i in range(4):
             here = pl.ds(pl.multiple_of(start + i * y_points, LANES), LANES)
             gx = metric_ref[0:1, here]
@@ -109,17 +113,19 @@
 
 
 def pick_edges(state_ref, edges_ref, border_ref, table_ref, picked_ref):
-    count = edges_ref.shape[0]
+    side = edges_ref.shape[1]
+    count = 2 * side
     to_rows(state_ref, 0, table_ref, 0, state_ref.shape[2])
 
     def step(i, _):
-        base = i * 16
-        places = [edges_ref[base + u] for u in range(16)]
-        for u in range(16):
-            picked_ref[pl.ds(base + u, 1), :] = table_ref[pl.ds(places[u], 1), :]
-        return 0
-
-    lax.fori_loop(0, count // 16, step, 0)
+        base = i * 8
+        places = [[edges_ref[k, base + u] for u in range(8)] for k in range(2)]
+        for k in range(2):
+            for u in range(8):
+                picked_ref[pl.ds(k * side + base + u, 1), :] = table_ref[pl.ds(places[k][u], 1), :]
+        return 0
+
+    lax.fori_loop(0, side // 8, step, 0)
     for c in range(count // LANES):
         block = from_rows(picked_ref, c * LANES, state_ref.shape[1])
         for f in range(3):
@@ -127,9 +133,9 @@
 
 
 def prepare_kernel(
-    n, x_points, y_points, surface_ref, rows_ref, state_ref, edges_ref, metric_ref, speed_ref,
+    n, x_points, y_points, rows_ref, state_ref, edges_ref, metric_ref, speed_ref,
     in_ref, stepped_ref, west_a_ref, east_a_ref, west_o_ref, east_o_ref,
-    terms_ref, out_ref, rim_ref, table_ref, picked_ref, send_sem, recv_sem, edge_send_sem, edge_recv_sem,
+    surface_ref, terms_ref, out_ref, rim_ref, table_ref, picked_ref, send_sem, recv_sem, edge_send_sem, edge_recv_sem,
 ):
     sec, dom = lax.axis_index("sec"), lax.axis_index("dom")
     right, left = lax.rem(dom + 1, n), lax.rem(dom + n - 1, n)
@@ -189,9 +195,13 @@
         for each in ocean_edges:
             each.start()
 
-    depth = surface_ref.shape[1]
-    for f in range(3):
-        terms_ref[f * depth : (f + 1) * depth, :] = two_terms(surface_ref[f])
+    depth, top = rows // LANES, state_ref.shape[1] - 1
+    for h in range(depth):
+        for f in range(3):
+            surface_ref[f * depth + h : f * depth + h + 1, :] = state_ref[
+                f, top : top + 1, h * LANES : (h + 1) * LANES
+            ]
+    terms_ref[...] = two_terms(surface_ref[...])
     per_peer = out_ref.shape[2]
 
     def copy(k):
@@ -241,37 +251,6 @@
             each.wait_send()
         ocean_edges[0].wait_recv()
         ocean_edges[1].wait_recv()
-
-
-def sweep_kernel(state_ref, west_ref, east_ref, adjacent_ref, kappa_ref, swept_ref, table_ref, sum_ref):
-    levels, rows, edge = state_ref.shape[1], state_ref.shape[2], west_ref.shape[2]
-    part = swept_ref.shape[2]
-    to_rows(state_ref, 0, table_ref, 0, rows)
-    to_rows(west_ref, 0, table_ref, rows, edge)
-    to_rows(east_ref, 0, table_ref, rows + edge, edge)
-
-    def step(i, _):
-        base = i * 16
-        places = [[adjacent_ref[base + (j * part + u)] for j in range(6)] for u in range(16)]
-        for u in range(16):
-            a = [table_ref[pl.ds(p, 1), :] for p in places[u]]
-            sum_ref[pl.ds(base + u, 1), :] = ((a[0] + a[1]) + (a[2] + a[3])) + (a[4] + a[5])
-        return 0
-
-    lax.fori_loop(0, part // 16, step, 0)
-    first = lax.axis_index("sec") * part
-
-    def finish(c, _):
-        here = pl.ds(pl.multiple_of(c * LANES, LANES), LANES)
-        there = pl.ds(pl.multiple_of(first + c * LANES, LANES), LANES)
-        block = from_rows(sum_ref, c * LANES, levels)
-        kappa = kappa_ref[0:1, here]
-        for f in range(3):
-            value = state_ref[f, :, there]
-            swept_ref[f, :, here] = value + kappa * (block[f] - 6.0 * value)
-        return 0
-
-    lax.fori_loop(0, part // LANES, finish, 0, unroll=4)
 
 
 def deinterleave(values, offset):
@@ -293,7 +272,16 @@
     return total
 
 
-def regrid_kernel(incoming_ref, source_ref, weight_ref, regrid_ref, terms_ref, index_ref, share_ref):
+def sweep_kernel(
+    state_ref, west_ref, east_ref, adjacent_ref, kappa_ref, incoming_ref, source_ref, weight_ref,
+    swept_ref, regrid_ref, table_ref, sum_ref, terms_ref, index_ref, share_ref,
+):
+    levels, rows, edge = state_ref.shape[1], state_ref.shape[2], west_ref.shape[2]
+    part = swept_ref.shape[2]
+    to_rows(state_ref, 0, table_ref, 0, rows)
+    to_rows(west_ref, 0, table_ref, rows, edge)
+    to_rows(east_ref, 0, table_ref, rows + edge, edge)
+
     depth = source_ref.shape[0]
     for f in range(3):
         table = incoming_ref[:, f].reshape(depth, LANES)
@@ -303,8 +291,16 @@
         index_ref[:, k * LANES : (k + 1) * LANES] = (deinterleave(source, k) + 0.5).astype(jnp.int32)
         share_ref[:, k * LANES : (k + 1) * LANES] = deinterleave(weight_ref[...], k)
 
+    steps = depth // 2
+    cells = part // steps
+
     def step(c, _):
         values = pick(terms_ref[...], depth, index_ref[pl.ds(c, 1), :])
+        for u in range(cells):
+            cell = c * cells + u
+            places = [adjacent_ref[c * cells + (j * part + u)] for j in range(6)]
+            a = [table_ref[pl.ds(p, 1), :] for p in places]
+            sum_ref[pl.ds(cell, 1), :] = ((a[0] + a[1]) + (a[2] + a[3])) + (a[4] + a[5])
         weight = share_ref[pl.ds(c, 1), :]
         whole = weight[:, :LANES] + weight[:, LANES:]
         here = pl.ds(pl.multiple_of(c * LANES, LANES), LANES)
@@ -313,7 +309,20 @@
             regrid_ref[f : f + 1, here] = (product[:, :LANES] + product[:, LANES:]) / whole
         return 0
 
-    lax.fori_loop(0, depth // 2, step, 0, unroll=4)
+    lax.fori_loop(0, steps, step, 0)
+    first = lax.axis_index("sec") * (part // LANES)
+
+    def finish(c, _):
+        here = pl.ds(pl.multiple_of(c * LANES, LANES), LANES)
+        there = pl.ds(pl.multiple_of((first + c) * LANES, LANES), LANES)
+        block = from_rows(sum_ref, c * LANES, levels)
+        kappa = kappa_ref[pl.ds(first + c, 1), :]
+        for f in range(3):
+            value = state_ref[f, :, there]
+            swept_ref[f, :, here] = value + kappa * (block[f] - 6.0 * value)
+        return 0
+
+    lax.fori_loop(0, part // LANES, finish, 0, unroll=4)
 
 
 def finish_kernel(
@@ -380,15 +389,15 @@
     ocean = lax.ppermute(state, "sec", [(1, 0)])
     ocean = jnp.where(sec == 0, ocean, state)
 
-    surface = state[:, levels - 1].reshape(3, rows // LANES, LANES)
     border = jax.ShapeDtypeStruct((3, levels, y_points), f32)
     arriving = jax.ShapeDtypeStruct((n, 3, cap // LANES, LANES), f32)
     incoming, stepped, west_a, east_a, west_o, east_o = pl.pallas_call(
         functools.partial(prepare_kernel, n, x_points, y_points),
         out_shape=[arriving, jax.ShapeDtypeStruct(state.shape, f32)] + [border] * 4,
-        in_specs=[VMEM] * 3 + [SMEM] + [VMEM] * 2,
+        in_specs=[VMEM] * 2 + [SMEM, VMEM, SMEM],
         out_specs=[VMEM] * 6,
         scratch_shapes=[
+            pltpu.VMEM((3 * rows // LANES, LANES), f32),
             pltpu.VMEM((3 * rows // LANES, 2 * LANES), jnp.bfloat16),
             pltpu.VMEM(arriving.shape, f32),
             pltpu.VMEM((3, levels, 2 * y_points), f32),
@@ -405,44 +414,33 @@
         ),
         name="prepare",
     )(
-        surface,
         send_rows.reshape(-1, LANES),
         state,
-        ocean_edges.reshape(-1),
+        ocean_edges,
         atm_metric,
-        jnp.broadcast_to(wave_speed[:, None], (levels, LANES)),
+        wave_speed,
     )
 
     adjacent = lax.dynamic_slice_in_dim(ocean_adjacent, sec * part, part, 1).reshape(-1)
-    kappa = lax.dynamic_slice_in_dim(ocean_kappa, sec * part, part, 0).reshape(1, -1)
-    swept = pl.pallas_call(
+    swept, regrid = pl.pallas_call(
         sweep_kernel,
-        out_shape=jax.ShapeDtypeStruct((3, levels, part), f32),
-        in_specs=[VMEM] * 3 + [SMEM, VMEM],
-        out_specs=VMEM,
+        out_shape=[jax.ShapeDtypeStruct((3, levels, part), f32), jax.ShapeDtypeStruct((3, rows), f32)],
+        in_specs=[VMEM] * 3 + [SMEM] + [VMEM] * 4,
+        out_specs=[VMEM] * 2,
         scratch_shapes=[
             pltpu.VMEM((rows + 2 * y_points, LANES), f32),
             pltpu.VMEM((part, LANES), f32),
-        ],
-        compiler_params=pltpu.CompilerParams(**PARAMS),
-        name="sweep",
-    )(ocean, west_o, east_o, adjacent, kappa)
-    helped = lax.ppermute(swept, "sec", [(0, 1)])
-
-    regrid = pl.pallas_call(
-        regrid_kernel,
-        out_shape=jax.ShapeDtypeStruct((3, rows), f32),
-        in_specs=[VMEM] * 3,
-        out_specs=VMEM,
-        scratch_shapes=[
             pltpu.VMEM((3 * slots // LANES, 2 * LANES), jnp.bfloat16),
             pltpu.VMEM((slots // LANES // 2, 2 * LANES), jnp.int32),
             pltpu.VMEM((slots // LANES // 2, 2 * LANES), f32),
         ],
         compiler_params=pltpu.CompilerParams(**PARAMS),
-        cost_estimate=pl.CostEstimate(flops=6 * LANES * slots * slots // LANES, bytes_accessed=slots * 20, transcendentals=0),
-        name="regrid",
-    )(incoming, intersection_source.reshape(-1, LANES), intersection_weight.reshape(-1, LANES))
+        name="sweep",
+    )(
+        ocean, west_o, east_o, adjacent, ocean_kappa.reshape(-1, LANES), incoming,
+        intersection_source.reshape(-1, LANES), intersection_weight.reshape(-1, LANES),
+    )
+    helped = lax.ppermute(swept, "sec", [(0, 1)])
 
     return pl.pallas_call(
         functools.partial(finish_kernel, x_points, y_points),

time: 61.1 us -> 55.8 us (0.913)
  Pallas kernels: 52.5 us -> 47.2 us
  waiting for transfers between devices: 0.01 us -> 1.31 us
  local copies, waits for them, and re-layouts: 4.58 us -> 3.37 us
    pallas_call x2 -> x1, Pallas kernels: 34.3 us -> 28.2 us  [body(): pl.pallas_call(sweep_kernel, out_shape=[jax.ShapeDtypeStruct((3, levels,...]
    ppermute x1, waiting for transfers between devices: 0.01 us -> 1.31 us  [body(): helped = lax.ppermute(swept, 'sec', [(0, 1)])]
    slice x1 -> x0, local copies, waits for them, and re-layouts: 1.22 us -> none  [body(): surface = state[:, levels - 1].reshape(3, rows // LANES, LANES)]
    pallas_call x1, Pallas kernels: 16.3 us -> 17.1 us  [body(): pl.pallas_call(functools.partial(prepare_kernel, n, x_points, y_points),...]
    unnamed x23 -> x22, local copies, waits for them, and re-layouts: 3.21 us -> 3.3 us
  transfers between devices with their start and end apart: 2 -> 2, of which waited for: 0 -> 1; matrix products, arithmetic and copies ran while one was open for 2% -> 0% of each run, Pallas kernels for 40% -> 31%
where the time goes in v4:
time: 55.8 us; the launch traced here: 55.6 us
  Pallas kernels  47.2 us (85%)
  starting transfers between devices  3.45 us (6%)
  local copies, waits for them, and re-layouts  3.37 us (6%)
  waiting for transfers between devices  1.31 us (2%)
    pallas_call x1, Pallas kernels, body(): pl.pallas_call(sweep_kernel, out_shape=[jax.ShapeDtypeStruct((3, levels,...  28.2 us
    pallas_call x1, Pallas kernels, body(): pl.pallas_call(functools.partial(prepare_kernel, n, x_points, y_points),...  17.1 us
    unnamed x22, local copies, waits for them, and re-layouts  3.3 us
    ppermute x1, starting transfers between devices, body(): helped = lax.ppermute(swept, 'sec', [(0, 1)])  2.04 us
    pallas_call x1, Pallas kernels, body(): pl.pallas_call(functools.partial(finish_kernel, x_points, y_points), out_...  1.92 us
    ppermute x1, starting transfers between devices, body(): ocean = lax.ppermute(state, 'sec', [(1, 0)])  1.41 us
    ppermute x1, waiting for transfers between devices, body(): helped = lax.ppermute(swept, 'sec', [(0, 1)])  1.31 us
  transfers between devices with their start and end apart: 2, of which 1 were waited for; matrix products, arithmetic and copies ran while one was open for 0% of the time, Pallas kernels for 31%

profile of v4, /device:TPU:0, one launch (start us, length us, event | category | flops | bytes accessed | tf_op | source)
XLA Modules:
  0.0 55.6 jit_solution(4511675229238484123)
XLA Ops:
  0.0 0.0 copy-start
  0.0 1.4 %collective-permute-start = (f32[3,8,8192]{2,1,0:T(8,128)}, f32[3,8,8192]{2,1,0:T(8,128)S(1)}, u32[]{:S(2)}, u32[]{:S(2)}) collective-permute-start(f32[3,8,8192]{2,1,0:T(8,128)} %state_ref.1), channel_id=1, source_target_pairs={{16,0},{17,1},{18,2},{19,3},{20,4},{21,5},{22,6},{23,7},{24,8},{25... | collective-permute-start | bytes 2359304 | tf_op jit(solution)/shard_map/ppermute | solution.py:389
  1.4 0.0 copy-done
  1.5 0.0 copy-start.7
  1.5 0.0 copy-start.8
  1.5 0.0 copy-start.9
  1.5 0.1 reshape.16.adjacent_ref
  1.6 0.0 copy-start.10
  1.6 0.7 %copy-done.7 = s32[16384]{0:T(1024)S(1)} copy-done((s32[16384]{0:T(1024)S(1)}, s32[16384]{0:T(1024)}, u32[]{:S(2)}) %copy-start.7) | copy-done | bytes 65560
  2.3 0.0 copy-done.8
  2.3 0.0 copy-done.9
  2.3 0.0 copy-done.10
  2.3 0.0 copy-start.1
  2.3 1.1 %copy-done.1 = f32[3,8,8192]{2,1,0:T(8,128)S(1)} copy-done((f32[3,8,8192]{2,1,0:T(8,128)S(1)}, f32[3,8,8192]{2,1,0:T(8,128)}, u32[]{:S(2)}) %copy-start.1) | copy-done | bytes 786456
  3.5 0.0 copy-start.2
  3.5 17.1 %prepare.1 = (f32[16,3,8,128]{3,2,1,0:T(8,128)S(1)}, f32[3,8,8192]{2,1,0:T(8,128)S(1)}, f32[3,8,512]{2,1,0:T(8,128)S(1)}, f32[3,8,512]{2,1,0:T(8,128)S(1)}, f32[...) custom-call(s32[128,128]{1,0:T(8,128)S(1)} %bitcast.7, f32[3,8,8192]{2,1,0:T(8,128)S(1)} %copy-done.1, ...), custom_call_target="tpu_custom_call" | custom-call | flops 805306368 | bytes 2359296 | tf_op jit(solution)/shard_map/prepare/pallas_call | solution.py:394
  20.6 0.0 copy-start.3
  20.6 0.0 copy-start.4
  20.6 0.0 collective-permute-done
  20.6 0.0 copy-done.2
  20.6 0.0 copy-start.5
  20.6 0.1 broadcast_select_fusion.state_ref
  20.7 0.7 %copy-done.3 = s32[16384]{0:T(1024)S(1)} copy-done((s32[16384]{0:T(1024)S(1)}, s32[16384]{0:T(1024)}, u32[]{:S(2)}) %copy-start.3) | copy-done | bytes 65560
  21.4 0.0 copy-done.4
  21.4 0.0 copy-done.5
  21.4 28.2 %sweep.1 = (f32[3,8,4096]{2,1,0:T(8,128)S(1)}, f32[3,8192]{1,0:T(4,128)S(1)}) custom-call(f32[3,8,8192]{2,1,0:T(8,128)S(1)} %broadcast_select_fusion.state_ref, f32[3,8,512]{2,1,0:T(8,128)S(1)} %get-tuple-element.13.west_ref, f32[3,8,512]{2,1,0:T(8,128)S(1)} %get-tuple-element.14.east_ref, s32[24576]{0:T(1024)S(1)} %reshape.16.adjacent_ref, ...), custom_call_target="tpu_custom_call" | custom-call | tf_op jit(solution)/shard_map/sweep/pallas_call | solution.py:425
  49.6 2.0 %collective-permute-start.1 = (f32[3,8,4096]{2,1,0:T(8,128)S(1)}, f32[3,8,4096]{2,1,0:T(8,128)S(1)}, u32[]{:S(2)}, u32[]{:S(2)}) collective-permute-start(f32[3,8,4096]{2,1,0:T(8,128)S(1)} %get-tuple-element.20.own_ref), channel_id=1, source_target_pairs={{0,16},{1,17},{2,18},{3,19},{4,20},{5,21},{6,22},{7,23},{8,24},{9,... | collective-permute-start | bytes 1179656 | tf_op jit(solution)/shard_map/ppermute | solution.py:443
  51.7 1.3 %collective-permute-done.1.helped_ref = f32[3,8,4096]{2,1,0:T(8,128)S(1)} collective-permute-done((f32[3,8,4096]{2,1,0:T(8,128)S(1)}, f32[3,8,4096]{2,1,0:T(8,128)S(1)}, u32[]{:S(2)}, u32[]{:S(2)}) %collective-permute-start.1) | collective-permute-done | bytes 393248 | tf_op jit(solution)/shard_map/ppermute | solution.py:443
  53.0 0.0 copy-start.6
  53.0 0.7 %copy-done.6 = f32[1,3]{1,0:T(1,128)S(1)} copy-done((f32[1,3]{1,0:T(1,128)S(1)}, f32[1,3]{1,0:T(1,128)}, u32[]{:S(2)}) %copy-start.6) | copy-done | bytes 36
  53.6 1.9 %finish.1 = f32[3,8,8192]{2,1,0:T(8,128)} custom-call(f32[3,8192]{1,0:T(4,128)S(1)} %get-tuple-element.16.regrid_ref, f32[1,3]{1,0:T(1,128)S(1)} %copy-done.6, f32[3,8,8192]{2,1,0:T(8,128)S(1)} %get-tuple-element.17.stepped_ref, f32[3,8,512]{2,1,0:T(8,128)S(1)} %get-tuple-element.18.west_ref, f32[3,8,512]{2,1,0:T(8,128)S(1)} %get-tuple-element.19.east_ref, ...), custom_call_target="tpu_custom_call" | custom-call | tf_op jit(solution)/shard_map/finish/pallas_call | solution.py:445
  (1 shorter events, 0.0 us)
Async XLA Ops:
  0.0 1.4 %copy-start = (s32[6,8192]{1,0:T(8,128)S(1)}, s32[6,8192]{1,0:T(8,128)}, u32[]{:S(2)}) copy-start(s32[6,8192]{1,0:T(8,128)} %param.17) | copy-start | bytes 589828
  0.0 20.6 %collective-permute-start = (f32[3,8,8192]{2,1,0:T(8,128)}, f32[3,8,8192]{2,1,0:T(8,128)S(1)}, u32[]{:S(2)}, u32[]{:S(2)}) collective-permute-start(f32[3,8,8192]{2,1,0:T(8,128)} %state_ref.1), channel_id=1, source_target_pairs={{16,0},{17,1},{18,2},{19,3},{20,4},{21,5},{22,6},{23,7},{24,8},{25... | collective-permute-start | bytes 2359304 | tf_op jit(solution)/shard_map/ppermute | solution.py:389
  1.5 0.8 %copy-start.7 = (s32[16384]{0:T(1024)S(1)}, s32[16384]{0:T(1024)}, u32[]{:S(2)}) copy-start(s32[16384]{0:T(1024)} %param.11) | copy-start | bytes 196612
  1.5 0.9 %copy-start.8 = (f32[2,8192]{1,0:T(2,128)S(1)}, f32[2,8192]{1,0:T(2,128)}, u32[]{:S(2)}) copy-start(f32[2,8192]{1,0:T(2,128)} %metric_ref.1) | copy-start | bytes 196612
  1.5 0.9 %copy-start.9 = (s32[2,512]{1,0:T(2,128)S(1)}, s32[2,512]{1,0:T(2,128)}, u32[]{:S(2)}) copy-start(s32[2,512]{1,0:T(2,128)} %edges_ref.1) | copy-start | bytes 12292
  1.6 0.8 %copy-start.10 = (f32[8]{0:T(128)S(1)}, f32[8]{0:T(128)}, u32[]{:S(2)}) copy-start(f32[8]{0:T(128)} %speed_ref.1) | copy-start | bytes 100
  2.3 1.1 %copy-start.1 = (f32[3,8,8192]{2,1,0:T(8,128)S(1)}, f32[3,8,8192]{2,1,0:T(8,128)}, u32[]{:S(2)}) copy-start(f32[3,8,8192]{2,1,0:T(8,128)} %state_ref.1) | copy-start | bytes 2359300
  3.5 17.1 %copy-start.2 = (f32[3,8,8192]{2,1,0:T(8,128)S(1)}, f32[3,8,8192]{2,1,0:T(8,128)}, u32[]{:S(2)}) copy-start(f32[3,8,8192]{2,1,0:T(8,128)} %state_ref.1) | copy-start | bytes 2359300
  20.6 0.8 %copy-start.3 = (s32[16384]{0:T(1024)S(1)}, s32[16384]{0:T(1024)}, u32[]{:S(2)}) copy-start(s32[16384]{0:T(1024)} %param.12) | copy-start | bytes 196612
  20.6 0.9 %copy-start.4 = (f32[16384]{0:T(1024)S(1)}, f32[16384]{0:T(1024)}, u32[]{:S(2)}) copy-start(f32[16384]{0:T(1024)} %param.13) | copy-start | bytes 196612
  20.6 0.8 %copy-start.5 = (f32[8192]{0:T(1024)S(1)}, f32[8192]{0:T(1024)}, u32[]{:S(2)}) copy-start(f32[8192]{0:T(1024)} %param.19) | copy-start | bytes 98308
  49.6 3.4 %collective-permute-start.1 = (f32[3,8,4096]{2,1,0:T(8,128)S(1)}, f32[3,8,4096]{2,1,0:T(8,128)S(1)}, u32[]{:S(2)}, u32[]{:S(2)}) collective-permute-start(f32[3,8,4096]{2,1,0:T(8,128)S(1)} %get-tuple-element.20.own_ref), channel_id=1, source_target_pairs={{0,16},{1,17},{2,18},{3,19},{4,20},{5,21},{6,22},{7,23},{8,24},{9,... | collective-permute-start | bytes 1179656 | tf_op jit(solution)/shard_map/ppermute | solution.py:443
  53.0 0.7 %copy-start.6 = (f32[1,3]{1,0:T(1,128)S(1)}, f32[1,3]{1,0:T(1,128)}, u32[]{:S(2)}) copy-start(f32[1,3]{1,0:T(1,128)} %rate_ref.1) | copy-start | bytes 40

commit v5 on v4

--- a/solution.py
+++ b/solution.py
@@ -134,7 +134,7 @@
 
 def prepare_kernel(
     n, x_points, y_points, rows_ref, state_ref, edges_ref, metric_ref, speed_ref,
-    in_ref, stepped_ref, west_a_ref, east_a_ref, west_o_ref, east_o_ref,
+    in_ref, stepped_ref, west_a_ref, east_a_ref, west_o_ref, east_o_ref, ocean_ref,
     surface_ref, terms_ref, out_ref, rim_ref, table_ref, picked_ref, send_sem, recv_sem, edge_send_sem, edge_recv_sem,
 ):
     sec, dom = lax.axis_index("sec"), lax.axis_index("dom")
@@ -179,6 +179,7 @@
         edge(1, rim_first, east_o_ref, 1, (1, left)),
         edge(2, rim_last, west_o_ref, 0, (0, right)),
         edge(3, rim_first, east_o_ref, 1, (0, left)),
+        edge(4, state_ref, ocean_ref, 4, (0, dom)),
     ]
     atmosphere_edges = [
         edge(0, stepped_ref.at[:, :, last], west_a_ref, 2, (0, right)),
@@ -244,6 +245,7 @@
             each.wait()
         ocean_edges[0].wait_recv()
         ocean_edges[1].wait_recv()
+        ocean_edges[4].wait_recv()
 
     @pl.when(sec == 1)
     def _():
@@ -386,16 +388,14 @@
     part = rows // 2
     f32 = jnp.float32
 
-    ocean = lax.ppermute(state, "sec", [(1, 0)])
-    ocean = jnp.where(sec == 0, ocean, state)
-
     border = jax.ShapeDtypeStruct((3, levels, y_points), f32)
+    whole = jax.ShapeDtypeStruct(state.shape, f32)
     arriving = jax.ShapeDtypeStruct((n, 3, cap // LANES, LANES), f32)
-    incoming, stepped, west_a, east_a, west_o, east_o = pl.pallas_call(
+    incoming, stepped, west_a, east_a, west_o, east_o, ocean = pl.pallas_call(
         functools.partial(prepare_kernel, n, x_points, y_points),
-        out_shape=[arriving, jax.ShapeDtypeStruct(state.shape, f32)] + [border] * 4,
+        out_shape=[arriving, whole] + [border] * 4 + [whole],
         in_specs=[VMEM] * 2 + [SMEM, VMEM, SMEM],
-        out_specs=[VMEM] * 6,
+        out_specs=[VMEM] * 7,
         scratch_shapes=[
             pltpu.VMEM((3 * rows // LANES, LANES), f32),
             pltpu.VMEM((3 * rows // LANES, 2 * LANES), jnp.bfloat16),
@@ -405,8 +405,8 @@
             pltpu.VMEM((2 * y_points, LANES), f32),
             pltpu.SemaphoreType.DMA((n,)),
             pltpu.SemaphoreType.DMA((n,)),
-            pltpu.SemaphoreType.DMA((4,)),
-            pltpu.SemaphoreType.DMA((4,)),
+            pltpu.SemaphoreType.DMA((5,)),
+            pltpu.SemaphoreType.DMA((5,)),
         ],
         compiler_params=pltpu.CompilerParams(collective_id=0, has_side_effects=True, **PARAMS),
         cost_estimate=pl.CostEstimate(
@@ -421,6 +421,7 @@
         wave_speed,
     )
 
+    ocean = jnp.where(sec == 0, ocean, state)
     adjacent = lax.dynamic_slice_in_dim(ocean_adjacent, sec * part, part, 1).reshape(-1)
     swept, regrid = pl.pallas_call(
         sweep_kernel,

time: 55.8 us -> 54 us (0.968)
  starting transfers between devices: 3.45 us -> 1.62 us
  Pallas kernels: 47.2 us -> 46.2 us
  local copies, waits for them, and re-layouts: 3.37 us -> 4.35 us
    ppermute x1 -> x0, starting transfers between devices: 1.41 us -> none  [body(): ocean = lax.ppermute(state, 'sec', [(1, 0)])]
    unnamed x22, local copies, waits for them, and re-layouts: 3.3 us -> 4.29 us
    pallas_call x1, Pallas kernels: 17.1 us -> 16.1 us  [body(): pl.pallas_call(functools.partial(prepare_kernel, n, x_points, y_points),...]
  transfers between devices with their start and end apart: 2 -> 1, of which waited for: 1 -> 1; matrix products, arithmetic and copies ran while one was open for 0% -> 0% of each run, Pallas kernels for 31% -> 0%
where the time goes in v5:
time: 54 us; the launch traced here: 53.7 us
  Pallas kernels  46.2 us (86%)
  local copies, waits for them, and re-layouts  4.35 us (8%)
  starting transfers between devices  1.62 us (3%)
  waiting for transfers between devices  1.31 us (2%)
    pallas_call x1, Pallas kernels, body(): pl.pallas_call(sweep_kernel, out_shape=[jax.ShapeDtypeStruct((3, levels,...  28.2 us
    pallas_call x1, Pallas kernels, body(): pl.pallas_call(functools.partial(prepare_kernel, n, x_points, y_points),...  16.1 us
    unnamed x22, local copies, waits for them, and re-layouts  4.29 us
    pallas_call x1, Pallas kernels, body(): pl.pallas_call(functools.partial(finish_kernel, x_points, y_points), out_...  1.92 us
    ppermute x1, starting transfers between devices, body(): helped = lax.ppermute(swept, 'sec', [(0, 1)])  1.62 us
    ppermute x1, waiting for transfers between devices, body(): helped = lax.ppermute(swept, 'sec', [(0, 1)])  1.31 us
  transfers between devices with their start and end apart: 1, of which 1 were waited for; matrix products, arithmetic and copies ran while one was open for 0% of the time, Pallas kernels for 0%

profile of v5, /device:TPU:0, one launch (start us, length us, event | category | flops | bytes accessed | tf_op | source)
XLA Modules:
  0.0 53.7 jit_solution(13047977903814825197)
XLA Ops:
  0.0 0.0 copy-start
  0.0 0.9 %copy-done = s32[6,8192]{1,0:T(8,128)S(1)} copy-done((s32[6,8192]{1,0:T(8,128)S(1)}, s32[6,8192]{1,0:T(8,128)}, u32[]{:S(2)}) %copy-start) | copy-done | bytes 196632
  1.0 0.0 copy-start.7
  1.0 0.0 copy-start.8
  1.0 0.0 copy-start.9
  1.0 0.1 reshape.16.adjacent_ref
  1.1 0.0 copy-start.10
  1.1 0.7 %copy-done.7 = s32[16384]{0:T(1024)S(1)} copy-done((s32[16384]{0:T(1024)S(1)}, s32[16384]{0:T(1024)}, u32[]{:S(2)}) %copy-start.7) | copy-done | bytes 65560
  1.8 0.0 copy-done.8
  1.8 0.0 copy-done.9
  1.8 0.0 copy-done.10
  1.8 0.0 copy-start.1
  1.8 1.1 %copy-done.1 = f32[3,8,8192]{2,1,0:T(8,128)S(1)} copy-done((f32[3,8,8192]{2,1,0:T(8,128)S(1)}, f32[3,8,8192]{2,1,0:T(8,128)}, u32[]{:S(2)}) %copy-start.1) | copy-done | bytes 786456
  3.0 0.0 copy-start.2
  3.0 16.1 %prepare.1 = (f32[16,3,8,128]{3,2,1,0:T(8,128)S(1)}, f32[3,8,8192]{2,1,0:T(8,128)S(1)}, f32[3,8,512]{2,1,0:T(8,128)S(1)}, f32[3,8,512]{2,1,0:T(8,128)S(1)}, f32[...) custom-call(s32[128,128]{1,0:T(8,128)S(1)} %bitcast.7, f32[3,8,8192]{2,1,0:T(8,128)S(1)} %copy-done.1, ...), custom_call_target="tpu_custom_call" | custom-call | flops 805306368 | bytes 2359296 | tf_op jit(solution)/shard_map/prepare/pallas_call | solution.py:394
  19.1 0.0 copy-done.2
  19.1 0.0 copy-start.3
  19.2 0.0 copy-start.4
  19.2 0.0 copy-start.5
  19.2 0.1 broadcast_select_fusion.state_ref
  19.3 0.7 %copy-done.3 = s32[16384]{0:T(1024)S(1)} copy-done((s32[16384]{0:T(1024)S(1)}, s32[16384]{0:T(1024)}, u32[]{:S(2)}) %copy-start.3) | copy-done | bytes 65560
  20.0 0.0 copy-done.4
  20.0 0.0 copy-done.5
  20.0 28.2 %sweep.1 = (f32[3,8,4096]{2,1,0:T(8,128)S(1)}, f32[3,8192]{1,0:T(4,128)S(1)}) custom-call(f32[3,8,8192]{2,1,0:T(8,128)S(1)} %broadcast_select_fusion.state_ref, f32[3,8,512]{2,1,0:T(8,128)S(1)} %get-tuple-element.15.west_ref, f32[3,8,512]{2,1,0:T(8,128)S(1)} %get-tuple-element.16.east_ref, s32[24576]{0:T(1024)S(1)} %reshape.16.adjacent_ref, ...), custom_call_target="tpu_custom_call" | custom-call | tf_op jit(solution)/shard_map/sweep/pallas_call | solution.py:426
  48.2 1.6 %collective-permute-start = (f32[3,8,4096]{2,1,0:T(8,128)S(1)}, f32[3,8,4096]{2,1,0:T(8,128)S(1)}, u32[]{:S(2)}, u32[]{:S(2)}) collective-permute-start(f32[3,8,4096]{2,1,0:T(8,128)S(1)} %get-tuple-element.22.own_ref), channel_id=1, source_target_pairs={{0,16},{1,17},{2,18},{3,19},{4,20},{5,21},{6,22},{7,23},{8,24},{9,... | collective-permute-start | bytes 1179656 | tf_op jit(solution)/shard_map/ppermute | solution.py:444
  49.8 1.3 %collective-permute-done.helped_ref = f32[3,8,4096]{2,1,0:T(8,128)S(1)} collective-permute-done((f32[3,8,4096]{2,1,0:T(8,128)S(1)}, f32[3,8,4096]{2,1,0:T(8,128)S(1)}, u32[]{:S(2)}, u32[]{:S(2)}) %collective-permute-start) | collective-permute-done | bytes 393248 | tf_op jit(solution)/shard_map/ppermute | solution.py:444
  51.1 0.0 copy-start.6
  51.1 0.7 %copy-done.6 = f32[1,3]{1,0:T(1,128)S(1)} copy-done((f32[1,3]{1,0:T(1,128)S(1)}, f32[1,3]{1,0:T(1,128)}, u32[]{:S(2)}) %copy-start.6) | copy-done | bytes 36
  51.8 1.9 %finish.1 = f32[3,8,8192]{2,1,0:T(8,128)} custom-call(f32[3,8192]{1,0:T(4,128)S(1)} %get-tuple-element.18.regrid_ref, f32[1,3]{1,0:T(1,128)S(1)} %copy-done.6, f32[3,8,8192]{2,1,0:T(8,128)S(1)} %get-tuple-element.19.stepped_ref, f32[3,8,512]{2,1,0:T(8,128)S(1)} %get-tuple-element.20.west_ref, f32[3,8,512]{2,1,0:T(8,128)S(1)} %get-tuple-element.21.east_ref, ...), custom_call_target="tpu_custom_call" | custom-call | tf_op jit(solution)/shard_map/finish/pallas_call | solution.py:446
  (1 shorter events, 0.0 us)
Async XLA Ops:
  0.0 1.0 %copy-start = (s32[6,8192]{1,0:T(8,128)S(1)}, s32[6,8192]{1,0:T(8,128)}, u32[]{:S(2)}) copy-start(s32[6,8192]{1,0:T(8,128)} %param.17) | copy-start | bytes 589828
  1.0 0.8 %copy-start.7 = (s32[16384]{0:T(1024)S(1)}, s32[16384]{0:T(1024)}, u32[]{:S(2)}) copy-start(s32[16384]{0:T(1024)} %param.11) | copy-start | bytes 196612
  1.0 0.9 %copy-start.8 = (f32[2,8192]{1,0:T(2,128)S(1)}, f32[2,8192]{1,0:T(2,128)}, u32[]{:S(2)}) copy-start(f32[2,8192]{1,0:T(2,128)} %metric_ref.1) | copy-start | bytes 196612
  1.0 0.9 %copy-start.9 = (s32[2,512]{1,0:T(2,128)S(1)}, s32[2,512]{1,0:T(2,128)}, u32[]{:S(2)}) copy-start(s32[2,512]{1,0:T(2,128)} %edges_ref.1) | copy-start | bytes 12292
  1.1 0.8 %copy-start.10 = (f32[8]{0:T(128)S(1)}, f32[8]{0:T(128)}, u32[]{:S(2)}) copy-start(f32[8]{0:T(128)} %speed_ref.1) | copy-start | bytes 100
  1.8 1.1 %copy-start.1 = (f32[3,8,8192]{2,1,0:T(8,128)S(1)}, f32[3,8,8192]{2,1,0:T(8,128)}, u32[]{:S(2)}) copy-start(f32[3,8,8192]{2,1,0:T(8,128)} %state_ref.1) | copy-start | bytes 2359300
  3.0 16.2 %copy-start.2 = (f32[3,8,8192]{2,1,0:T(8,128)S(1)}, f32[3,8,8192]{2,1,0:T(8,128)}, u32[]{:S(2)}) copy-start(f32[3,8,8192]{2,1,0:T(8,128)} %state_ref.1) | copy-start | bytes 2359300
  19.1 0.8 %copy-start.3 = (s32[16384]{0:T(1024)S(1)}, s32[16384]{0:T(1024)}, u32[]{:S(2)}) copy-start(s32[16384]{0:T(1024)} %param.12) | copy-start | bytes 196612
  19.2 0.9 %copy-start.4 = (f32[16384]{0:T(1024)S(1)}, f32[16384]{0:T(1024)}, u32[]{:S(2)}) copy-start(f32[16384]{0:T(1024)} %param.13) | copy-start | bytes 196612
  19.2 0.9 %copy-start.5 = (f32[8192]{0:T(1024)S(1)}, f32[8192]{0:T(1024)}, u32[]{:S(2)}) copy-start(f32[8192]{0:T(1024)} %param.19) | copy-start | bytes 98308
  48.2 2.9 %collective-permute-start = (f32[3,8,4096]{2,1,0:T(8,128)S(1)}, f32[3,8,4096]{2,1,0:T(8,128)S(1)}, u32[]{:S(2)}, u32[]{:S(2)}) collective-permute-start(f32[3,8,4096]{2,1,0:T(8,128)S(1)} %get-tuple-element.22.own_ref), channel_id=1, source_target_pairs={{0,16},{1,17},{2,18},{3,19},{4,20},{5,21},{6,22},{7,23},{8,24},{9,... | collective-permute-start | bytes 1179656 | tf_op jit(solution)/shard_map/ppermute | solution.py:444
  51.1 0.7 %copy-start.6 = (f32[1,3]{1,0:T(1,128)S(1)}, f32[1,3]{1,0:T(1,128)}, u32[]{:S(2)}) copy-start(f32[1,3]{1,0:T(1,128)} %rate_ref.1) | copy-start | bytes 40
